TPU v7x, 32 devices: a whole 2x2x4 slice. The times are simulated.
32 devices in a mesh: layer: 2 (over x), row: 4 (over y, core), col: 4 (over z).
Axes of the slice: x: 2, y: 2, z: 4, core: 2. Of those that a mesh axis runs over, the one named last changes fastest.
Arguments:
- lower_inverse: bfloat16 [2, 4096, 4096], P('layer', 'row', 'col')
- upper_inverse: bfloat16 [2, 4096, 4096], P('layer', 'col', 'row')
- lower_coupling: bfloat16 [2, 4096, 8192], P('layer', 'row', 'col'), may hold values from -0.0625 to 0.0625
- upper_coupling: bfloat16 [2, 4096, 8192], P('layer', 'row', 'col'), may hold values from -0.0625 to 0.0625
- separator_lower: bfloat16 [8192, 8192], P(('layer', 'row'), 'col')
- separator_upper: bfloat16 [8192, 8192], P('col', ('layer', 'row'))
- subtree_rhs: float32 [2, 4096, 512], P('layer', 'col', 'row'), may hold values from -6 to 6
- separator_rhs: float32 [8192, 512], P('col', ('layer', 'row')), may hold values from -6 to 6
- column_counts: int32 [2], P('layer'), may hold values from 1024 to 4096, as said below
Outputs:
- subtree_solution: float32 [2, 4096, 512], P('layer', 'col', 'row')
- separator_solution: float32 [8192, 512], P('col', ('layer', 'row'))
Inputs may be any that keep to these rules, and one draw needn't show every extreme that they name: `column_counts`: each count is a multiple of 128.
All inputs are finite; a program needn't handle non-finite values.
Results may differ from a plain program's by a relative error of at most 0.019.
Values may be sent and summed in bfloat16 or wider, within the bound.
No kernel may reach another device: no remote copies, remote signals or barrier semaphores. Data moves between devices by JAX's collectives and lax.ppermute only.
A program may use at most 64 MiB of HBM per device.

v0:
```python
import jax
import jax.numpy as jnp
from jax import lax
from jax.sharding import PartitionSpec as P


def shards(
    lower_inverse,
    upper_inverse,
    lower_coupling,
    upper_coupling,
    separator_lower,
    separator_upper,
    subtree_rhs,
    separator_rhs,
    column_counts,
):
    col_limit = column_counts[0]
    rhs_full = lax.all_gather(subtree_rhs.astype(jnp.bfloat16), "row", axis=2, tiled=True).astype(
        subtree_rhs.dtype
    )[0]
    row_count = lower_inverse.shape[1]
    col_count = lower_inverse.shape[2]
    col_mask = (
        lax.axis_index("col") * col_count + lax.iota(jnp.int32, col_count) < col_limit
    ).astype(jnp.float32)[:, None]
    row_mask = (
        lax.axis_index("row") * row_count + lax.iota(jnp.int32, row_count) < col_limit
    ).astype(jnp.float32)[:, None]
    masked = (rhs_full * col_mask).astype(jnp.bfloat16)
    forward_part = jnp.dot(lower_inverse[0], masked, preferred_element_type=jnp.float32)
    forward = lax.psum(forward_part.astype(jnp.bfloat16), "col").astype(jnp.float32) * row_mask
    forward_low = forward.astype(jnp.bfloat16)
    share_width = separator_rhs.shape[1]
    share_index = lax.axis_index("layer") * lax.axis_size("row") + lax.axis_index("row")
    padded = lax.dynamic_update_slice(
        jnp.zeros((separator_rhs.shape[0], rhs_full.shape[1]), jnp.float32),
        separator_rhs,
        (jnp.int32(0), share_index * share_width),
    )
    update = lax.dot_general(
        lower_coupling[0], forward_low, (((0,), (0,)), ((), ())), preferred_element_type=jnp.float32
    )
    reduced_term = padded - update
    shares = lax.psum_scatter(
        reduced_term, ("layer", "row"), scatter_dimension=1, tiled=True
    ).astype(jnp.bfloat16)
    middle_part = jnp.dot(
        separator_lower,
        lax.all_gather(shares, ("layer", "row"), axis=1, tiled=True),
        preferred_element_type=jnp.float32,
    )
    middle = lax.psum(middle_part.astype(jnp.bfloat16), "col")
    back_term = jnp.dot(separator_upper, middle, preferred_element_type=jnp.float32)
    separator_solution = lax.psum_scatter(
        back_term, ("layer", "row"), scatter_dimension=1, tiled=True
    )
    coupled_part = jnp.dot(
        upper_coupling[0],
        lax.all_gather(
            separator_solution.astype(jnp.bfloat16), ("layer", "row"), axis=1, tiled=True
        ),
        preferred_element_type=jnp.float32,
    )
    coupled = lax.psum(coupled_part.astype(jnp.bfloat16), "col").astype(jnp.float32)
    interior = ((forward - coupled) * row_mask).astype(jnp.bfloat16)
    back_part = jnp.dot(upper_inverse[0], interior, preferred_element_type=jnp.float32)
    shares_back = lax.psum_scatter(
        back_part.astype(jnp.bfloat16), "row", scatter_dimension=1, tiled=True
    ).astype(jnp.float32)
    return ((shares_back * col_mask)[None], separator_solution)


def solution(mesh):
    placed = (
        P("layer", "row", "col"),
        P("layer", "col", "row"),
        P("layer", "row", "col"),
        P("layer", "row", "col"),
        P(("layer", "row"), "col"),
        P("col", ("layer", "row")),
        P("layer", "col", "row"),
        P("col", ("layer", "row")),
        P("layer"),
    )
    return jax.shard_map(
        shards,
        mesh=mesh,
        in_specs=placed,
        out_specs=(P("layer", "col", "row"), P("col", ("layer", "row"))),
        check_vma=False,
    )
```

profile of v0, /device:TPU:0, one launch (start us, length us, event | category | flops | bytes accessed | tf_op | source)
XLA Modules:
  0.0 416.3 jit_solution(10991359654763667624)
XLA Ops:
  7.2 1.9 convert_element_type.71
  9.2 0.0 all-reduce.4.cloned.1.call-start
  9.9 19.8 %all-gather.4.cloned.1.call-done = bf16[1,1024,512]{2,1,0:T(8,128)(2,1)} async-done(((bf16[1,1024,128]{2,1,0:T(8,128)(2,1)}), bf16[1,1024,512]{2,1,0:T(8,128)(2,1)}) %all-gather.4.cloned.1.call-update) | async-done | bytes 1048592 | tf_op jit(solution)/shard_map/all_gather | solution.py:19
  29.7 3.7 fusion.27
  33.6 2.5 broadcast_in_dim.8
  36.0 0.8 constant_dynamic-update-slice_fusion
  36.9 48.6 %all-reduce.4.cloned.1.call-done = bf16[1024,512]{0,1:T(8,128)(2,1)} async-done(((bf16[1024,512]{0,1:T(8,128)(2,1)}), bf16[1024,512]{0,1:T(8,128)(2,1)}) %all-reduce.4.cloned.1.call-update) | async-done | bytes 1048592 | tf_op jit(solution)/shard_map/psum | solution.py:32
  85.5 8.1 %bitcast_subtract_fusion = f32[2048,512]{0,1:T(8,128)} fusion(f32[2048,512]{0,1:T(8,128)} %constant_dynamic-update-slice_fusion, bf16[1,1024,2048]{2,1,0:T(8,128)(2,1)} %param.11, bf16[1024,512]{0,1:T(8,128)(2,1)} %all-reduce.4.cloned.1.call-done, f32[1024]{0:T(1024)S(1)} %fusion.37), kind=kOutput, calls=%fused_computation.2 | convolution fusion | flops 2150105088 | bytes 13635584 | tf_op jit(solution)/shard_map/dot_general | solution.py:41
  93.6 50.8 %reduce-scatter.4.cloned.1.call-done = f32[2048,64]{0,1:T(8,128)} async-done(((f32[2048,512]{0,1:T(8,128)}), f32[2048,64]{0,1:T(8,128)}) %reduce-scatter.4.cloned.1.call-update) | async-done | bytes 524304 | tf_op jit(solution)/shard_map/reduce_scatter | solution.py:45
  144.4 1.8 convert_element_type.81
  146.2 0.0 all-reduce.6.cloned.1.call-start
  146.3 28.4 %all-gather.6.cloned.1.call-done = bf16[2048,512]{0,1:T(8,128)(2,1)} async-done(((bf16[2048,64]{0,1:T(8,128)(2,1)}), bf16[2048,512]{0,1:T(8,128)(2,1)}) %all-gather.6.cloned.1.call-update) | async-done | bytes 2097168 | tf_op jit(solution)/shard_map/all_gather | solution.py:50
  174.7 6.2 %fusion.20 = bf16[1024,512]{0,1:T(8,128)(2,1)} fusion(bf16[2048,512]{0,1:T(8,128)(2,1)} %all-gather.6.cloned.1.call-done, bf16[1024,2048]{1,0:T(8,128)(2,1)} %param.13), kind=kOutput, calls=%fused_computation.18 | convolution fusion | flops 2148007936 | bytes 7340032 | tf_op jit(solution)/shard_map/dot_general | solution.py:48
  180.9 51.9 %all-reduce.6.cloned.1.call-done = bf16[1024,512]{0,1:T(8,128)(2,1)} async-done(((bf16[1024,512]{0,1:T(8,128)(2,1)}), bf16[1024,512]{0,1:T(8,128)(2,1)}) %all-reduce.6.cloned.1.call-update) | async-done | bytes 1048592 | tf_op jit(solution)/shard_map/psum | solution.py:53
  232.8 6.8 %convolution_bitcast_fusion = f32[2048,512]{0,1:T(8,128)} fusion(bf16[1024,512]{0,1:T(8,128)(2,1)} %all-reduce.6.cloned.1.call-done, bf16[2048,1024]{1,0:T(8,128)(2,1)} %param.14), kind=kOutput, calls=%fused_computation.5 | convolution fusion | flops 2147483648 | bytes 9437184 | tf_op jit(solution)/shard_map/dot_general | solution.py:54
  239.7 50.8 %reduce-scatter.6.cloned.1.call-done = f32[2048,64]{0,1:T(8,128)} async-done(((f32[2048,512]{0,1:T(8,128)}), f32[2048,64]{0,1:T(8,128)}) %reduce-scatter.6.cloned.1.call-update) | async-done | bytes 524304 | tf_op jit(solution)/shard_map/reduce_scatter | solution.py:55
  290.6 1.8 convert_element_type.84
  292.4 28.5 %all-gather.8.cloned.1.call-done = bf16[2048,512]{0,1:T(8,128)(2,1)} async-done(((bf16[2048,64]{0,1:T(8,128)(2,1)}), bf16[2048,512]{0,1:T(8,128)(2,1)}) %all-gather.8.cloned.1.call-update) | async-done | bytes 2097168 | tf_op jit(solution)/shard_map/all_gather | solution.py:60
  321.0 6.2 %fusion.21 = bf16[1024,512]{0,1:T(8,128)(2,1)} fusion(bf16[2048,512]{0,1:T(8,128)(2,1)} %all-gather.8.cloned.1.call-done, bf16[1,1024,2048]{2,1,0:T(8,128)(2,1)} %param.12), kind=kOutput, calls=%fused_computation.19 | convolution fusion | flops 2148007936 | bytes 7340032 | tf_op jit(solution)/shard_map/dot_general | solution.py:58
  327.2 51.9 %all-reduce.8.cloned.1.call-done = bf16[1024,512]{0,1:T(8,128)(2,1)} async-done(((bf16[1024,512]{0,1:T(8,128)(2,1)}), bf16[1024,512]{0,1:T(8,128)(2,1)}) %all-reduce.8.cloned.1.call-update) | async-done | bytes 1048592 | tf_op jit(solution)/shard_map/psum | solution.py:65
  379.1 4.2 %fusion.24 = bf16[1024,512]{0,1:T(8,128)(2,1)} fusion(bf16[1,1024,1024]{2,1,0:T(8,128)(2,1)} %param.10, bf16[1024,512]{0,1:T(8,128)(2,1)} %all-reduce.8.cloned.1.call-done, bf16[1024,512]{0,1:T(8,128)(2,1)S(1)} %copy-done.2, f32[1024]{0:T(1024)S(1)} %fusion.37), kind=kOutput, calls=%fused_computation.20 | convolution fusion | flops 1077411840 | bytes 5246976 | tf_op jit(solution)/shard_map/dot_general | solution.py:67
  383.4 24.4 %reduce-scatter.8.cloned.1.call-done = bf16[1024,128]{0,1:T(8,128)(2,1)} async-done(((bf16[1024,512]{0,1:T(8,128)(2,1)}), bf16[1024,128]{0,1:T(8,128)(2,1)}) %reduce-scatter.8.cloned.1.call-update) | async-done | bytes 262160 | tf_op jit(solution)/shard_map/reduce_scatter | solution.py:68
  407.8 1.0 multiply_bitcast_fusion
  408.8 1.0 copy.11
  (24 shorter events, 0.5 us)
Async XLA Ops:
  7.2 22.6 %copy-start = (bf16[1,1024,1024]{2,1,0:T(8,128)(2,1)S(1)}, bf16[1,1024,1024]{2,1,0:T(8,128)(2,1)}, u32[]{:S(2)}) copy-start(bf16[1,1024,1024]{2,1,0:T(8,128)(2,1)} %param.9) | copy-start | bytes 6291460
  7.2 22.5 %all-gather.4.cloned.1.call-start = ((), (), s32[]{:S(2)}) async-start(), calls=%async_computation.3 | async-start | bytes 1310720 | tf_op jit(solution)/shard_map/all_gather | solution.py:19
  9.2 76.3 %all-reduce.4.cloned.1.call-start = ((), (), s32[]{:S(2)}) async-start(), calls=%async_computation.4 | async-start | bytes 2097152 | tf_op jit(solution)/shard_map/psum | solution.py:32
  33.5 111.0 %reduce-scatter.4.cloned.1.call-start = ((), (), s32[]{:S(2)}) async-start(), calls=%async_computation.5 | async-start | bytes 4718592 | tf_op jit(solution)/shard_map/reduce_scatter | solution.py:45
  33.6 2.5 copy-start.1
  93.5 81.1 %all-gather.6.cloned.1.call-start = ((), (), s32[]{:S(2)}) async-start(), calls=%async_computation.6 | async-start | bytes 2359296 | tf_op jit(solution)/shard_map/all_gather | solution.py:50
  146.2 86.6 %all-reduce.6.cloned.1.call-start = ((), (), s32[]{:S(2)}) async-start(), calls=%async_computation.7 | async-start | bytes 2097152 | tf_op jit(solution)/shard_map/psum | solution.py:53
  180.9 109.7 %reduce-scatter.6.cloned.1.call-start = ((), (), s32[]{:S(2)}) async-start(), calls=%async_computation.8 | async-start | bytes 4718592 | tf_op jit(solution)/shard_map/reduce_scatter | solution.py:55
  239.7 81.3 %all-gather.8.cloned.1.call-start = ((), (), s32[]{:S(2)}) async-start(), calls=%async_computation.9 | async-start | bytes 2359296 | tf_op jit(solution)/shard_map/all_gather | solution.py:60
  292.4 86.7 %copy-start.2 = (bf16[1024,512]{0,1:T(8,128)(2,1)S(1)}, bf16[1024,512]{0,1:T(8,128)(2,1)}, u32[]{:S(2)}) copy-start(bf16[1024,512]{0,1:T(8,128)(2,1)} %all-reduce.4.cloned.1.call-done) | copy-start | bytes 3145732
  292.4 86.7 %all-reduce.8.cloned.1.call-start = ((), (), s32[]{:S(2)}) async-start(), calls=%async_computation.10 | async-start | bytes 2097152 | tf_op jit(solution)/shard_map/psum | solution.py:65
  327.1 80.7 %reduce-scatter.8.cloned.1.call-start = ((), (), s32[]{:S(2)}) async-start(), calls=%async_computation.11 | async-start | bytes 1310720 | tf_op jit(solution)/shard_map/reduce_scatter | solution.py:68
Sparse Core Ops, SparseCore 0:
  10.1 19.5 all-gather.3
  33.6 51.8 all-reduce.3
  93.7 50.7 reduce-scatter.3
  146.8 27.8 all-gather.5
  181.0 51.8 all-reduce.5
  239.8 50.7 reduce-scatter.5
  293.1 27.8 all-gather.7
  327.3 51.8 all-reduce.7
  383.5 24.2 reduce-scatter.7
where the time goes:
time: 417 us; the launch traced here: 416 us
  waiting for transfers between devices  355 us (85%)
  matrix products  35.2 us (8%)
  between operations  14.6 us (4%)
  other arithmetic  6.45 us (2%)
  local copies, waits for them, and re-layouts  4.33 us (1%)
    psum x1, waiting for transfers between devices, shards(): lax.psum(coupled_part.astype(jnp.bfloat16), 'col').astype(jnp.float32)  51.9 us
    psum x1, waiting for transfers between devices, shards(): middle = lax.psum(middle_part.astype(jnp.bfloat16), 'col')  51.9 us
    reduce_scatter x1, waiting for transfers between devices, shards(): lax.psum_scatter(back_term, ('layer', 'row'), scatter_dimension=1, tiled=...  50.8 us
    reduce_scatter x1, waiting for transfers between devices, shards(): lax.psum_scatter(reduced_term, ('layer', 'row'), scatter_dimension=1, til...  50.8 us
    psum x1, waiting for transfers between devices, shards(): lax.psum(forward_part.astype(jnp.bfloat16), 'col').astype(jnp.float32)  48.6 us
    all_gather x1, waiting for transfers between devices, shards(): lax.all_gather(separator_solution.astype(jnp.bfloat16), ('layer', 'row'),...  28.5 us
    all_gather x1, waiting for transfers between devices, shards(): lax.all_gather(shares, ('layer', 'row'), axis=1, tiled=True)  28.4 us
    reduce_scatter x1, waiting for transfers between devices, shards(): lax.psum_scatter(back_part.astype(jnp.bfloat16), 'row', scatter_dimension...  24.4 us
  transfers between devices with their start and end apart: 9, of which 9 were waited for; matrix products, arithmetic and copies ran while one was open for 1% of the time, Pallas kernels for 0%

commit v1 on v0

v1 whole, which is shorter than its diff:
```python
import jax
import jax.numpy as jnp
from jax import lax
from jax.sharding import PartitionSpec as P

F32 = jnp.float32
BF16 = jnp.bfloat16


def pick(array, index):
    return lax.dynamic_index_in_dim(array, index, 0, keepdims=False)


def place(parts):
    out = jnp.zeros((len(parts),) + parts[0][1].shape, parts[0][1].dtype)
    for index, block in parts:
        out = lax.dynamic_update_index_in_dim(out, block, index, 0)
    return out


def dot_nt(a, b):
    return lax.dot_general(a, b, (((1,), (1,)), ((), ())), preferred_element_type=F32)


def solution(mesh):
    layers, rows, cols = (mesh.shape[name] for name in ("layer", "row", "col"))
    pair = 2 if rows % 2 == 0 else 1
    high = rows // pair
    groups = layers * high

    def send_col(block, step):
        return lax.ppermute(block, "col", [(i, (i + step) % cols) for i in range(cols)])

    def send_high(block, step):
        return lax.ppermute(
            block,
            "row",
            [(i, (i // pair + step) % high * pair + i % pair) for i in range(rows)],
        )

    def send_pair(block):
        return lax.ppermute(block, "row", [(i, i ^ 1) for i in range(rows)])

    def send_group(block, step):
        return lax.ppermute(
            block,
            ("layer", "row"),
            [
                (i, (i // pair + step) % groups * pair + i % pair)
                for i in range(layers * rows)
            ],
        )

    def scatter(part, me, size, send):
        total = pick(part, me)
        low = part.astype(BF16)
        got = [send(pick(low, (me + k) % size), k) for k in range(1, size)]
        for block in got:
            total = total + block.astype(F32)
        return total

    def gather(block, me, size, send):
        return place(
            [(me, block)] + [((me - k) % size, send(block, k)) for k in range(1, size)]
        )

    def pair_scatter(part, core):
        if pair == 1:
            return part[:, 0]
        mine = lax.dynamic_index_in_dim(part, core, 1, keepdims=False)
        other = lax.dynamic_index_in_dim(part, 1 - core, 1, keepdims=False)
        return mine + send_pair(other.astype(BF16)).astype(F32)

    def pair_gather(block, core):
        if pair == 1:
            return block[:, None]
        out = jnp.zeros((block.shape[0], pair) + block.shape[1:], block.dtype)
        out = lax.dynamic_update_index_in_dim(out, block, core, 1)
        return lax.dynamic_update_index_in_dim(out, send_pair(block), 1 - core, 1)

    def shards(
        lower_inverse,
        upper_inverse,
        lower_coupling,
        upper_coupling,
        separator_lower,
        separator_upper,
        subtree_rhs,
        separator_rhs,
        column_counts,
    ):
        limit = column_counts[0]
        row_count = lower_inverse.shape[1]
        col_count = lower_inverse.shape[2]
        sep_count, width = separator_rhs.shape
        chunks = 2 if width % 32 == 0 else 1
        part = width // chunks
        total = layers * rows * part
        layer, row, col = (lax.axis_index(name) for name in ("layer", "row", "col"))
        core, up = row % pair, row // pair
        group = layer * high + up
        col_mask = (col * col_count + lax.iota(jnp.int32, col_count) < limit).astype(F32)
        row_mask = (row * row_count + lax.iota(jnp.int32, row_count) < limit).astype(F32)

        def col_scatter(x):
            return scatter(x.reshape(cols, -1, x.shape[1]), col, cols, send_col)

        def col_gather(x):
            return gather(x, col, cols, send_col).reshape(total, -1)

        def all_scatter(x):
            n = x.shape[1]
            mine = pair_scatter(x.reshape(groups, pair, part, n), core)
            return scatter(mine, group, groups, send_group)

        def all_gather(x):
            mine = gather(x, group, groups, send_group)
            return pair_gather(mine, core).reshape(total, -1)

        def row_gather(x):
            return pair_gather(gather(x, up, high, send_high), core).reshape(total, -1)

        def row_scatter(x):
            n = x.shape[1]
            mine = pair_scatter(x.reshape(high, pair, -1, n), core)
            return scatter(mine, up, high, send_high)

        given = (subtree_rhs[0] * col_mask[:, None]).astype(BF16).T
        given = given.reshape(layers, chunks, part, col_count)
        sep_given = separator_rhs.T.reshape(chunks, part, sep_count)

        solved, middles = [], []
        for h in range(chunks):
            masked = row_gather(given[:, h].reshape(layers * part, col_count))
            forward = col_scatter(dot_nt(masked, lower_inverse[0])) * row_mask
            update = jnp.dot(
                col_gather(forward.astype(BF16)),
                lower_coupling[0],
                preferred_element_type=F32,
            )
            reduced = all_gather((sep_given[h] - all_scatter(update)).astype(BF16))
            middle = col_gather(col_scatter(dot_nt(reduced, separator_lower)).astype(BF16))
            spread = all_scatter(dot_nt(middle, separator_upper))
            coupled = col_scatter(
                dot_nt(all_gather(spread.astype(BF16)), upper_coupling[0])
            )
            interior = col_gather(((forward - coupled) * row_mask).astype(BF16))
            back = row_scatter(dot_nt(interior, upper_inverse[0])) * col_mask
            middles.append(spread)
            solved.append(back.reshape(layers, 1, part, col_count))
        out = jnp.concatenate(solved, axis=1).reshape(layers * width, col_count).T
        return out[None], jnp.concatenate(middles, axis=0).T

    placed = (
        P("layer", "row", "col"),
        P("layer", "col", "row"),
        P("layer", "row", "col"),
        P("layer", "row", "col"),
        P(("layer", "row"), "col"),
        P("col", ("layer", "row")),
        P("layer", "col", "row"),
        P("col", ("layer", "row")),
        P("layer"),
    )
    return jax.shard_map(
        shards,
        mesh=mesh,
        in_specs=placed,
        out_specs=(P("layer", "col", "row"), P("col", ("layer", "row"))),
        check_vma=False,
    )
```

time: 417 us -> 230 us (0.55)
  waiting for transfers between devices: 355 us -> 83.2 us
  starting transfers between devices: 0.37 us -> 122 us
  matrix products: 35.2 us -> 13.3 us
  between operations: 14.6 us -> 2.95 us
    psum x3 -> x0, waiting for transfers between devices: 152 us -> none  [the longest x1 51.9 us: shards(): lax.psum(coupled_part.astype(jnp.bfloat16), 'col').astype(jnp.float32)]
    reduce_scatter x3 -> x0, waiting for transfers between devices: 126 us -> none  [the longest x1 50.8 us: shards(): lax.psum_scatter(back_term, ('layer', 'row'), scatter_dimension=1, tiled=...]
    ppermute x0 -> x76, starting transfers between devices: none -> 122 us  [the longest x36 81.3 us: send_col(): lax.ppermute(block, 'col', [(i, (i + step) % cols) for i in range(cols)])]
    ppermute x0 -> x76, waiting for transfers between devices: none -> 83.2 us  [the longest x36 53.9 us: send_col(): lax.ppermute(block, 'col', [(i, (i + step) % cols) for i in range(cols)])]
    all_gather x3 -> x0, waiting for transfers between devices: 76.7 us -> none  [the longest x1 28.5 us: shards(): lax.all_gather(separator_solution.astype(jnp.bfloat16), ('layer', 'row'),...]
    dot_general x6 -> x12, matrix products: 35.2 us -> 13.3 us  [the longest x10 10.7 us: dot_nt(): lax.dot_general(a, b, (((1,), (1,)), ((), ())), preferred_element_type=F32)]
    convert_element_type x5 -> x7, other arithmetic: 5.46 us -> 0.82 us  [the longest x4 0.77 us: scatter(): low = part.astype(BF16)]
  transfers between devices with their start and end apart: 9 -> 76, of which waited for: 9 -> 30; matrix products, arithmetic and copies ran while one was open for 1% -> 8% of each run, Pallas kernels for 0% -> 0%
where the time goes in v1:
time: 230 us; the launch traced here: 229 us
  starting transfers between devices  122 us (53%)
  waiting for transfers between devices  83.2 us (36%)
  matrix products  13.3 us (6%)
  local copies, waits for them, and re-layouts  5.16 us (2%)
  between operations  2.95 us (1%)
  other arithmetic  2.86 us (1%)
    ppermute x36, starting transfers between devices, send_col(): lax.ppermute(block, 'col', [(i, (i + step) % cols) for i in range(cols)])  81.3 us
    ppermute x36, waiting for transfers between devices, send_col(): lax.ppermute(block, 'col', [(i, (i + step) % cols) for i in range(cols)])  53.9 us
    ppermute x24, starting transfers between devices, send_group(): lax.ppermute(block, ('layer', 'row'), [(i, (i // pair + step) % groups *...  33 us
    ppermute x24, waiting for transfers between devices, send_group(): lax.ppermute(block, ('layer', 'row'), [(i, (i // pair + step) % groups *...  18.7 us
    dot_general x10, matrix products, dot_nt(): lax.dot_general(a, b, (((1,), (1,)), ((), ())), preferred_element_type=F32)  10.7 us
    ppermute x4, waiting for transfers between devices, send_high(): lax.ppermute(block, 'row', [(i, (i // pair + step) % high * pair + i % pa...  10.5 us
    ppermute x4, starting transfers between devices, send_high(): lax.ppermute(block, 'row', [(i, (i // pair + step) % high * pair + i % pa...  6.3 us
  transfers between devices with their start and end apart: 76, of which 30 were waited for; matrix products, arithmetic and copies ran while one was open for 8% of the time, Pallas kernels for 0%

profile of v1, /device:TPU:0, one launch (start us, length us, event | category | flops | bytes accessed | tf_op | source)
XLA Modules:
  0.0 229.3 jit_solution(203729170273809351)
XLA Ops:
  2.8 3.0 %collective-permute-start = (bf16[64,1024]{1,0:T(8,128)(2,1)S(1)}, bf16[64,1024]{1,0:T(8,128)(2,1)S(1)}, u32[]{:S(2)}, u32[]{:S(2)}) collective-permute-start(bf16[64,1024]{1,0:T(8,128)(2,1)S(1)} %bitcast.444), channel_id=1, source_target_pairs={{0,8},{4,12},{8,0},{12,4},{1,9},{5,13},{9,1},{13,5},{2,10},{6,14},... | collective-permute-start | bytes 393224 | tf_op jit(solution)/shard_map/ppermute | solution.py:35
  6.3 3.8 %collective-permute-done = bf16[64,1024]{1,0:T(8,128)(2,1)S(1)} collective-permute-done((bf16[64,1024]{1,0:T(8,128)(2,1)S(1)}, bf16[64,1024]{1,0:T(8,128)(2,1)S(1)}, u32[]{:S(2)}, u32[]{:S(2)}) %collective-permute-start) | collective-permute-done | bytes 131104 | tf_op jit(solution)/shard_map/ppermute | solution.py:35
  23.6 3.6 %collective-permute-done.3 = bf16[64,1024]{1,0:T(8,128)(2,1)S(1)} collective-permute-done((bf16[64,1024]{1,0:T(8,128)(2,1)S(1)}, bf16[64,1024]{1,0:T(8,128)(2,1)S(1)}, u32[]{:S(2)}, u32[]{:S(2)}) %collective-permute-start.3) | collective-permute-done | bytes 131104 | tf_op jit(solution)/shard_map/ppermute | solution.py:32
  27.4 9.0 %collective-permute-start.5 = (bf16[64,1024]{1,0:T(8,128)(2,1)S(1)}, bf16[64,1024]{1,0:T(8,128)(2,1)S(1)}, u32[]{:S(2)}, u32[]{:S(2)}) collective-permute-start(bf16[64,1024]{1,0:T(8,128)(2,1)S(1)} %get-tuple-element.18), channel_id=1, source_target_pairs={{0,1},{1,2},{2,3},{3,0},{4,5},{5,6},{6,7},{7,4},{8,9},{9,10},{10,1... | collective-permute-start | bytes 393224 | tf_op jit(solution)/shard_map/ppermute | solution.py:32
  38.8 4.2 %collective-permute-done.41 = bf16[64,1024]{1,0:T(8,128)(2,1)S(1)} collective-permute-done((bf16[64,1024]{1,0:T(8,128)(2,1)S(1)}, bf16[64,1024]{1,0:T(8,128)(2,1)S(1)}, u32[]{:S(2)}, u32[]{:S(2)}) %collective-permute-start.41) | collective-permute-done | bytes 131104 | tf_op jit(solution)/shard_map/ppermute | solution.py:32
  43.2 4.1 %collective-permute-start.43 = (bf16[64,1024]{1,0:T(8,128)(2,1)S(1)}, bf16[64,1024]{1,0:T(8,128)(2,1)S(1)}, u32[]{:S(2)}, u32[]{:S(2)}) collective-permute-start(bf16[64,1024]{1,0:T(8,128)(2,1)S(1)} %get-tuple-element.33), channel_id=1, source_target_pairs={{0,1},{1,2},{2,3},{3,0},{4,5},{5,6},{6,7},{7,4},{8,9},{9,10},{10,1... | collective-permute-start | bytes 393224 | tf_op jit(solution)/shard_map/ppermute | solution.py:32
  49.7 5.2 %collective-permute-done.6 = bf16[64,1024]{1,0:T(8,128)(2,1)S(1)} collective-permute-done((bf16[64,1024]{1,0:T(8,128)(2,1)S(1)}, bf16[64,1024]{1,0:T(8,128)(2,1)S(1)}, u32[]{:S(2)}, u32[]{:S(2)}) %collective-permute-start.6) | collective-permute-done | bytes 131104 | tf_op jit(solution)/shard_map/ppermute | solution.py:32
  56.5 4.1 %collective-permute-done.44 = bf16[64,1024]{1,0:T(8,128)(2,1)S(1)} collective-permute-done((bf16[64,1024]{1,0:T(8,128)(2,1)S(1)}, bf16[64,1024]{1,0:T(8,128)(2,1)S(1)}, u32[]{:S(2)}, u32[]{:S(2)}) %collective-permute-start.44) | collective-permute-done | bytes 131104 | tf_op jit(solution)/shard_map/ppermute | solution.py:32
  71.3 3.4 %collective-permute-done.11 = bf16[32,2048]{1,0:T(8,128)(2,1)S(1)} collective-permute-done((bf16[32,2048]{1,0:T(8,128)(2,1)S(1)}, bf16[32,2048]{1,0:T(8,128)(2,1)S(1)}, u32[]{:S(2)}, u32[]{:S(2)}) %collective-permute-start.11) | collective-permute-done | bytes 131104 | tf_op jit(solution)/shard_map/ppermute | solution.py:45
  91.0 3.3 %collective-permute-start.16 = (bf16[64,1024]{1,0:T(8,128)(2,1)S(1)}, bf16[64,1024]{1,0:T(8,128)(2,1)S(1)}, u32[]{:S(2)}, u32[]{:S(2)}) collective-permute-start(bf16[64,1024]{1,0:T(8,128)(2,1)S(1)} %get-tuple-element.40), channel_id=1, source_target_pairs={{0,1},{1,2},{2,3},{3,0},{4,5},{5,6},{6,7},{7,4},{8,9},{9,10},{10,1... | collective-permute-start | bytes 393224 | tf_op jit(solution)/shard_map/ppermute | solution.py:32
  102.4 3.0 %collective-permute-done.17 = bf16[64,1024]{1,0:T(8,128)(2,1)S(1)} collective-permute-done((bf16[64,1024]{1,0:T(8,128)(2,1)S(1)}, bf16[64,1024]{1,0:T(8,128)(2,1)S(1)}, u32[]{:S(2)}, u32[]{:S(2)}) %collective-permute-start.17) | collective-permute-done | bytes 131104 | tf_op jit(solution)/shard_map/ppermute | solution.py:32
  105.6 9.0 %collective-permute-start.19 = (bf16[64,1024]{1,0:T(8,128)(2,1)S(1)}, bf16[64,1024]{1,0:T(8,128)(2,1)S(1)}, u32[]{:S(2)}, u32[]{:S(2)}) collective-permute-start(bf16[64,1024]{1,0:T(8,128)(2,1)S(1)} %get-tuple-element.12), channel_id=1, source_target_pairs={{0,1},{1,2},{2,3},{3,0},{4,5},{5,6},{6,7},{7,4},{8,9},{9,10},{10,1... | collective-permute-start | bytes 393224 | tf_op jit(solution)/shard_map/ppermute | solution.py:32
  117.1 5.0 %collective-permute-done.55 = bf16[64,1024]{1,0:T(8,128)(2,1)S(1)} collective-permute-done((bf16[64,1024]{1,0:T(8,128)(2,1)S(1)}, bf16[64,1024]{1,0:T(8,128)(2,1)S(1)}, u32[]{:S(2)}, u32[]{:S(2)}) %collective-permute-start.55) | collective-permute-done | bytes 131104 | tf_op jit(solution)/shard_map/ppermute | solution.py:32
  122.2 3.4 %collective-permute-start.57 = (bf16[64,1024]{1,0:T(8,128)(2,1)S(1)}, bf16[64,1024]{1,0:T(8,128)(2,1)S(1)}, u32[]{:S(2)}, u32[]{:S(2)}) collective-permute-start(bf16[64,1024]{1,0:T(8,128)(2,1)S(1)} %get-tuple-element.27), channel_id=1, source_target_pairs={{0,1},{1,2},{2,3},{3,0},{4,5},{5,6},{6,7},{7,4},{8,9},{9,10},{10,1... | collective-permute-start | bytes 393224 | tf_op jit(solution)/shard_map/ppermute | solution.py:32
  128.1 5.2 %collective-permute-done.20 = bf16[64,1024]{1,0:T(8,128)(2,1)S(1)} collective-permute-done((bf16[64,1024]{1,0:T(8,128)(2,1)S(1)}, bf16[64,1024]{1,0:T(8,128)(2,1)S(1)}, u32[]{:S(2)}, u32[]{:S(2)}) %collective-permute-start.20) | collective-permute-done | bytes 131104 | tf_op jit(solution)/shard_map/ppermute | solution.py:32
  134.9 4.1 %collective-permute-done.58 = bf16[64,1024]{1,0:T(8,128)(2,1)S(1)} collective-permute-done((bf16[64,1024]{1,0:T(8,128)(2,1)S(1)}, bf16[64,1024]{1,0:T(8,128)(2,1)S(1)}, u32[]{:S(2)}, u32[]{:S(2)}) %collective-permute-start.58) | collective-permute-done | bytes 131104 | tf_op jit(solution)/shard_map/ppermute | solution.py:32
  149.7 3.4 %collective-permute-done.25 = bf16[32,2048]{1,0:T(8,128)(2,1)S(1)} collective-permute-done((bf16[32,2048]{1,0:T(8,128)(2,1)S(1)}, bf16[32,2048]{1,0:T(8,128)(2,1)S(1)}, u32[]{:S(2)}, u32[]{:S(2)}) %collective-permute-start.25) | collective-permute-done | bytes 131104 | tf_op jit(solution)/shard_map/ppermute | solution.py:45
  168.9 3.3 %collective-permute-start.30 = (bf16[64,1024]{1,0:T(8,128)(2,1)S(1)}, bf16[64,1024]{1,0:T(8,128)(2,1)S(1)}, u32[]{:S(2)}, u32[]{:S(2)}) collective-permute-start(bf16[64,1024]{1,0:T(8,128)(2,1)S(1)} %get-tuple-element.34), channel_id=1, source_target_pairs={{0,1},{1,2},{2,3},{3,0},{4,5},{5,6},{6,7},{7,4},{8,9},{9,10},{10,1... | collective-permute-start | bytes 393224 | tf_op jit(solution)/shard_map/ppermute | solution.py:32
  180.1 3.2 %collective-permute-done.31 = bf16[64,1024]{1,0:T(8,128)(2,1)S(1)} collective-permute-done((bf16[64,1024]{1,0:T(8,128)(2,1)S(1)}, bf16[64,1024]{1,0:T(8,128)(2,1)S(1)}, u32[]{:S(2)}, u32[]{:S(2)}) %collective-permute-start.31) | collective-permute-done | bytes 131104 | tf_op jit(solution)/shard_map/ppermute | solution.py:32
  183.5 9.0 %collective-permute-start.33 = (bf16[64,1024]{1,0:T(8,128)(2,1)S(1)}, bf16[64,1024]{1,0:T(8,128)(2,1)S(1)}, u32[]{:S(2)}, u32[]{:S(2)}) collective-permute-start(bf16[64,1024]{1,0:T(8,128)(2,1)S(1)} %get-tuple-element.5), channel_id=1, source_target_pairs={{0,1},{1,2},{2,3},{3,0},{4,5},{5,6},{6,7},{7,4},{8,9},{9,10},{10,1... | collective-permute-start | bytes 393224 | tf_op jit(solution)/shard_map/ppermute | solution.py:32
  194.9 4.9 %collective-permute-done.69 = bf16[64,1024]{1,0:T(8,128)(2,1)S(1)} collective-permute-done((bf16[64,1024]{1,0:T(8,128)(2,1)S(1)}, bf16[64,1024]{1,0:T(8,128)(2,1)S(1)}, u32[]{:S(2)}, u32[]{:S(2)}) %collective-permute-start.69) | collective-permute-done | bytes 131104 | tf_op jit(solution)/shard_map/ppermute | solution.py:32
  200.1 3.4 %collective-permute-start.71 = (bf16[64,1024]{1,0:T(8,128)(2,1)S(1)}, bf16[64,1024]{1,0:T(8,128)(2,1)S(1)}, u32[]{:S(2)}, u32[]{:S(2)}) collective-permute-start(bf16[64,1024]{1,0:T(8,128)(2,1)S(1)} %get-tuple-element.20), channel_id=1, source_target_pairs={{0,1},{1,2},{2,3},{3,0},{4,5},{5,6},{6,7},{7,4},{8,9},{9,10},{10,1... | collective-permute-start | bytes 393224 | tf_op jit(solution)/shard_map/ppermute | solution.py:32
  206.0 5.1 %collective-permute-done.34 = bf16[64,1024]{1,0:T(8,128)(2,1)S(1)} collective-permute-done((bf16[64,1024]{1,0:T(8,128)(2,1)S(1)}, bf16[64,1024]{1,0:T(8,128)(2,1)S(1)}, u32[]{:S(2)}, u32[]{:S(2)}) %collective-permute-start.34) | collective-permute-done | bytes 131104 | tf_op jit(solution)/shard_map/ppermute | solution.py:32
  211.1 5.6 %collective-permute-done.72 = bf16[64,1024]{1,0:T(8,128)(2,1)S(1)} collective-permute-done((bf16[64,1024]{1,0:T(8,128)(2,1)S(1)}, bf16[64,1024]{1,0:T(8,128)(2,1)S(1)}, u32[]{:S(2)}, u32[]{:S(2)}) %collective-permute-start.72) | collective-permute-done | bytes 131104 | tf_op jit(solution)/shard_map/ppermute | solution.py:32
  (263 shorter events, 114.8 us)
Async XLA Ops:
  19.7 18.3 %collective-permute-start.40 = (bf16[64,1024]{1,0:T(8,128)(2,1)S(1)}, bf16[64,1024]{1,0:T(8,128)(2,1)S(1)}, u32[]{:S(2)}, u32[]{:S(2)}) collective-permute-start(bf16[64,1024]{1,0:T(8,128)(2,1)S(1)} %get-tuple-element.61), channel_id=1, source_target_pairs={{0,1},{1,2},{2,3},{3,0},{4,5},{5,6},{6,7},{7,4},{8,9},{9,10},{10,1... | collective-permute-start | bytes 393224 | tf_op jit(solution)/shard_map/ppermute | solution.py:32
  20.5 22.6 %collective-permute-start.41 = (bf16[64,1024]{1,0:T(8,128)(2,1)S(1)}, bf16[64,1024]{1,0:T(8,128)(2,1)S(1)}, u32[]{:S(2)}, u32[]{:S(2)}) collective-permute-start(bf16[64,1024]{1,0:T(8,128)(2,1)S(1)} %get-tuple-element.63), channel_id=1, source_target_pairs={{0,2},{1,3},{2,0},{3,1},{4,6},{5,7},{6,4},{7,5},{8,10},{9,11},{10,... | collective-permute-start | bytes 393224 | tf_op jit(solution)/shard_map/ppermute | solution.py:32
  21.6 21.5 %collective-permute-start.42 = (bf16[64,1024]{1,0:T(8,128)(2,1)S(1)}, bf16[64,1024]{1,0:T(8,128)(2,1)S(1)}, u32[]{:S(2)}, u32[]{:S(2)}) collective-permute-start(bf16[64,1024]{1,0:T(8,128)(2,1)S(1)} %get-tuple-element.62), channel_id=1, source_target_pairs={{0,3},{1,0},{2,1},{3,2},{4,7},{5,4},{6,5},{7,6},{8,11},{9,8},{10,9... | collective-permute-start | bytes 393224 | tf_op jit(solution)/shard_map/ppermute | solution.py:32
  27.4 19.9 %collective-permute-start.5 = (bf16[64,1024]{1,0:T(8,128)(2,1)S(1)}, bf16[64,1024]{1,0:T(8,128)(2,1)S(1)}, u32[]{:S(2)}, u32[]{:S(2)}) collective-permute-start(bf16[64,1024]{1,0:T(8,128)(2,1)S(1)} %get-tuple-element.18), channel_id=1, source_target_pairs={{0,1},{1,2},{2,3},{3,0},{4,5},{5,6},{6,7},{7,4},{8,9},{9,10},{10,1... | collective-permute-start | bytes 393224 | tf_op jit(solution)/shard_map/ppermute | solution.py:32
  36.4 18.6 %collective-permute-start.6 = (bf16[64,1024]{1,0:T(8,128)(2,1)S(1)}, bf16[64,1024]{1,0:T(8,128)(2,1)S(1)}, u32[]{:S(2)}, u32[]{:S(2)}) collective-permute-start(bf16[64,1024]{1,0:T(8,128)(2,1)S(1)} %get-tuple-element.18), channel_id=1, source_target_pairs={{0,2},{1,3},{2,0},{3,1},{4,6},{5,7},{6,4},{7,5},{8,10},{9,11},{10,... | collective-permute-start | bytes 393224 | tf_op jit(solution)/shard_map/ppermute | solution.py:32
  38.0 17.0 %collective-permute-start.7 = (bf16[64,1024]{1,0:T(8,128)(2,1)S(1)}, bf16[64,1024]{1,0:T(8,128)(2,1)S(1)}, u32[]{:S(2)}, u32[]{:S(2)}) collective-permute-start(bf16[64,1024]{1,0:T(8,128)(2,1)S(1)} %get-tuple-element.18), channel_id=1, source_target_pairs={{0,3},{1,0},{2,1},{3,2},{4,7},{5,4},{6,5},{7,6},{8,11},{9,8},{10,9... | collective-permute-start | bytes 393224 | tf_op jit(solution)/shard_map/ppermute | solution.py:32
  43.2 13.2 %collective-permute-start.43 = (bf16[64,1024]{1,0:T(8,128)(2,1)S(1)}, bf16[64,1024]{1,0:T(8,128)(2,1)S(1)}, u32[]{:S(2)}, u32[]{:S(2)}) collective-permute-start(bf16[64,1024]{1,0:T(8,128)(2,1)S(1)} %get-tuple-element.33), channel_id=1, source_target_pairs={{0,1},{1,2},{2,3},{3,0},{4,5},{5,6},{6,7},{7,4},{8,9},{9,10},{10,1... | collective-permute-start | bytes 393224 | tf_op jit(solution)/shard_map/ppermute | solution.py:32
  47.3 13.3 %collective-permute-start.44 = (bf16[64,1024]{1,0:T(8,128)(2,1)S(1)}, bf16[64,1024]{1,0:T(8,128)(2,1)S(1)}, u32[]{:S(2)}, u32[]{:S(2)}) collective-permute-start(bf16[64,1024]{1,0:T(8,128)(2,1)S(1)} %get-tuple-element.33), channel_id=1, source_target_pairs={{0,2},{1,3},{2,0},{3,1},{4,6},{5,7},{6,4},{7,5},{8,10},{9,11},{10,... | collective-permute-start | bytes 393224 | tf_op jit(solution)/shard_map/ppermute | solution.py:32
  47.3 13.3 %collective-permute-start.45 = (bf16[64,1024]{1,0:T(8,128)(2,1)S(1)}, bf16[64,1024]{1,0:T(8,128)(2,1)S(1)}, u32[]{:S(2)}, u32[]{:S(2)}) collective-permute-start(bf16[64,1024]{1,0:T(8,128)(2,1)S(1)} %get-tuple-element.33), channel_id=1, source_target_pairs={{0,3},{1,0},{2,1},{3,2},{4,7},{5,4},{6,5},{7,6},{8,11},{9,8},{10,9... | collective-permute-start | bytes 393224 | tf_op jit(solution)/shard_map/ppermute | solution.py:32
  98.2 16.4 %collective-permute-start.54 = (bf16[64,1024]{1,0:T(8,128)(2,1)S(1)}, bf16[64,1024]{1,0:T(8,128)(2,1)S(1)}, u32[]{:S(2)}, u32[]{:S(2)}) collective-permute-start(bf16[64,1024]{1,0:T(8,128)(2,1)S(1)} %get-tuple-element.55), channel_id=1, source_target_pairs={{0,1},{1,2},{2,3},{3,0},{4,5},{5,6},{6,7},{7,4},{8,9},{9,10},{10,1... | collective-permute-start | bytes 393224 | tf_op jit(solution)/shard_map/ppermute | solution.py:32
  99.4 22.7 %collective-permute-start.55 = (bf16[64,1024]{1,0:T(8,128)(2,1)S(1)}, bf16[64,1024]{1,0:T(8,128)(2,1)S(1)}, u32[]{:S(2)}, u32[]{:S(2)}) collective-permute-start(bf16[64,1024]{1,0:T(8,128)(2,1)S(1)} %get-tuple-element.57), channel_id=1, source_target_pairs={{0,2},{1,3},{2,0},{3,1},{4,6},{5,7},{6,4},{7,5},{8,10},{9,11},{10,... | collective-permute-start | bytes 393224 | tf_op jit(solution)/shard_map/ppermute | solution.py:32
  100.7 21.3 %collective-permute-start.56 = (bf16[64,1024]{1,0:T(8,128)(2,1)S(1)}, bf16[64,1024]{1,0:T(8,128)(2,1)S(1)}, u32[]{:S(2)}, u32[]{:S(2)}) collective-permute-start(bf16[64,1024]{1,0:T(8,128)(2,1)S(1)} %get-tuple-element.56), channel_id=1, source_target_pairs={{0,3},{1,0},{2,1},{3,2},{4,7},{5,4},{6,5},{7,6},{8,11},{9,8},{10,9... | collective-permute-start | bytes 393224 | tf_op jit(solution)/shard_map/ppermute | solution.py:32
  105.6 20.1 %collective-permute-start.19 = (bf16[64,1024]{1,0:T(8,128)(2,1)S(1)}, bf16[64,1024]{1,0:T(8,128)(2,1)S(1)}, u32[]{:S(2)}, u32[]{:S(2)}) collective-permute-start(bf16[64,1024]{1,0:T(8,128)(2,1)S(1)} %get-tuple-element.12), channel_id=1, source_target_pairs={{0,1},{1,2},{2,3},{3,0},{4,5},{5,6},{6,7},{7,4},{8,9},{9,10},{10,1... | collective-permute-start | bytes 393224 | tf_op jit(solution)/shard_map/ppermute | solution.py:32
  114.6 18.7 %collective-permute-start.20 = (bf16[64,1024]{1,0:T(8,128)(2,1)S(1)}, bf16[64,1024]{1,0:T(8,128)(2,1)S(1)}, u32[]{:S(2)}, u32[]{:S(2)}) collective-permute-start(bf16[64,1024]{1,0:T(8,128)(2,1)S(1)} %get-tuple-element.12), channel_id=1, source_target_pairs={{0,2},{1,3},{2,0},{3,1},{4,6},{5,7},{6,4},{7,5},{8,10},{9,11},{10,... | collective-permute-start | bytes 393224 | tf_op jit(solution)/shard_map/ppermute | solution.py:32
  114.6 18.7 %collective-permute-start.21 = (bf16[64,1024]{1,0:T(8,128)(2,1)S(1)}, bf16[64,1024]{1,0:T(8,128)(2,1)S(1)}, u32[]{:S(2)}, u32[]{:S(2)}) collective-permute-start(bf16[64,1024]{1,0:T(8,128)(2,1)S(1)} %get-tuple-element.12), channel_id=1, source_target_pairs={{0,3},{1,0},{2,1},{3,2},{4,7},{5,4},{6,5},{7,6},{8,11},{9,8},{10,9... | collective-permute-start | bytes 393224 | tf_op jit(solution)/shard_map/ppermute | solution.py:32
  125.6 13.3 %collective-permute-start.58 = (bf16[64,1024]{1,0:T(8,128)(2,1)S(1)}, bf16[64,1024]{1,0:T(8,128)(2,1)S(1)}, u32[]{:S(2)}, u32[]{:S(2)}) collective-permute-start(bf16[64,1024]{1,0:T(8,128)(2,1)S(1)} %get-tuple-element.27), channel_id=1, source_target_pairs={{0,2},{1,3},{2,0},{3,1},{4,6},{5,7},{6,4},{7,5},{8,10},{9,11},{10,... | collective-permute-start | bytes 393224 | tf_op jit(solution)/shard_map/ppermute | solution.py:32
  125.6 13.3 %collective-permute-start.59 = (bf16[64,1024]{1,0:T(8,128)(2,1)S(1)}, bf16[64,1024]{1,0:T(8,128)(2,1)S(1)}, u32[]{:S(2)}, u32[]{:S(2)}) collective-permute-start(bf16[64,1024]{1,0:T(8,128)(2,1)S(1)} %get-tuple-element.27), channel_id=1, source_target_pairs={{0,3},{1,0},{2,1},{3,2},{4,7},{5,4},{6,5},{7,6},{8,11},{9,8},{10,9... | collective-permute-start | bytes 393224 | tf_op jit(solution)/shard_map/ppermute | solution.py:32
  176.1 16.4 %collective-permute-start.68 = (bf16[64,1024]{1,0:T(8,128)(2,1)S(1)}, bf16[64,1024]{1,0:T(8,128)(2,1)S(1)}, u32[]{:S(2)}, u32[]{:S(2)}) collective-permute-start(bf16[64,1024]{1,0:T(8,128)(2,1)S(1)} %get-tuple-element.49), channel_id=1, source_target_pairs={{0,1},{1,2},{2,3},{3,0},{4,5},{5,6},{6,7},{7,4},{8,9},{9,10},{10,1... | collective-permute-start | bytes 393224 | tf_op jit(solution)/shard_map/ppermute | solution.py:32
  177.2 22.7 %collective-permute-start.69 = (bf16[64,1024]{1,0:T(8,128)(2,1)S(1)}, bf16[64,1024]{1,0:T(8,128)(2,1)S(1)}, u32[]{:S(2)}, u32[]{:S(2)}) collective-permute-start(bf16[64,1024]{1,0:T(8,128)(2,1)S(1)} %get-tuple-element.51), channel_id=1, source_target_pairs={{0,2},{1,3},{2,0},{3,1},{4,6},{5,7},{6,4},{7,5},{8,10},{9,11},{10,... | collective-permute-start | bytes 393224 | tf_op jit(solution)/shard_map/ppermute | solution.py:32
  178.6 21.2 %collective-permute-start.70 = (bf16[64,1024]{1,0:T(8,128)(2,1)S(1)}, bf16[64,1024]{1,0:T(8,128)(2,1)S(1)}, u32[]{:S(2)}, u32[]{:S(2)}) collective-permute-start(bf16[64,1024]{1,0:T(8,128)(2,1)S(1)} %get-tuple-element.50), channel_id=1, source_target_pairs={{0,3},{1,0},{2,1},{3,2},{4,7},{5,4},{6,5},{7,6},{8,11},{9,8},{10,9... | collective-permute-start | bytes 393224 | tf_op jit(solution)/shard_map/ppermute | solution.py:32
  183.5 20.1 %collective-permute-start.33 = (bf16[64,1024]{1,0:T(8,128)(2,1)S(1)}, bf16[64,1024]{1,0:T(8,128)(2,1)S(1)}, u32[]{:S(2)}, u32[]{:S(2)}) collective-permute-start(bf16[64,1024]{1,0:T(8,128)(2,1)S(1)} %get-tuple-element.5), channel_id=1, source_target_pairs={{0,1},{1,2},{2,3},{3,0},{4,5},{5,6},{6,7},{7,4},{8,9},{9,10},{10,1... | collective-permute-start | bytes 393224 | tf_op jit(solution)/shard_map/ppermute | solution.py:32
  192.5 18.6 %collective-permute-start.34 = (bf16[64,1024]{1,0:T(8,128)(2,1)S(1)}, bf16[64,1024]{1,0:T(8,128)(2,1)S(1)}, u32[]{:S(2)}, u32[]{:S(2)}) collective-permute-start(bf16[64,1024]{1,0:T(8,128)(2,1)S(1)} %get-tuple-element.5), channel_id=1, source_target_pairs={{0,2},{1,3},{2,0},{3,1},{4,6},{5,7},{6,4},{7,5},{8,10},{9,11},{10,... | collective-permute-start | bytes 393224 | tf_op jit(solution)/shard_map/ppermute | solution.py:32
  192.5 24.2 %collective-permute-start.35 = (bf16[64,1024]{1,0:T(8,128)(2,1)S(1)}, bf16[64,1024]{1,0:T(8,128)(2,1)S(1)}, u32[]{:S(2)}, u32[]{:S(2)}) collective-permute-start(bf16[64,1024]{1,0:T(8,128)(2,1)S(1)} %get-tuple-element.5), channel_id=1, source_target_pairs={{0,3},{1,0},{2,1},{3,2},{4,7},{5,4},{6,5},{7,6},{8,11},{9,8},{10,9... | collective-permute-start | bytes 393224 | tf_op jit(solution)/shard_map/ppermute | solution.py:32
  203.5 13.2 %collective-permute-start.73 = (bf16[64,1024]{1,0:T(8,128)(2,1)S(1)}, bf16[64,1024]{1,0:T(8,128)(2,1)S(1)}, u32[]{:S(2)}, u32[]{:S(2)}) collective-permute-start(bf16[64,1024]{1,0:T(8,128)(2,1)S(1)} %get-tuple-element.20), channel_id=1, source_target_pairs={{0,3},{1,0},{2,1},{3,2},{4,7},{5,4},{6,5},{7,6},{8,11},{9,8},{10,9... | collective-permute-start | bytes 393224 | tf_op jit(solution)/shard_map/ppermute | solution.py:32
  (60 other events, 557.7 us)

commit v2 on v1

--- a/solution.py
+++ b/solution.py
@@ -64,6 +64,22 @@
             [(me, block)] + [((me - k) % size, send(block, k)) for k in range(1, size)]
         )
 
+    def swap_col(block, bits):
+        return lax.ppermute(block, "col", [(i, i ^ bits) for i in range(cols)])
+
+    def line_scatter(part, me):
+        low = part.astype(BF16)
+        far = swap_col(pick(low, me ^ 2), 1)
+        near = swap_col(pick(low, me ^ 1), 1)
+        across = swap_col((pick(part, me ^ 3) + far.astype(F32)).astype(BF16), 3)
+        return pick(part, me) + near.astype(F32) + across.astype(F32)
+
+    def line_gather(block, me):
+        across = swap_col(block, 3)
+        near = swap_col(block, 1)
+        far = swap_col(across, 1)
+        return place([(me, block), (me ^ 1, near), (me ^ 3, across), (me ^ 2, far)])
+
     def pair_scatter(part, core):
         if pair == 1:
             return part[:, 0]
@@ -103,9 +119,14 @@
         row_mask = (row * row_count + lax.iota(jnp.int32, row_count) < limit).astype(F32)
 
         def col_scatter(x):
-            return scatter(x.reshape(cols, -1, x.shape[1]), col, cols, send_col)
+            pieces = x.reshape(cols, -1, x.shape[1])
+            if cols == 4:
+                return line_scatter(pieces, col)
+            return scatter(pieces, col, cols, send_col)
 
         def col_gather(x):
+            if cols == 4:
+                return line_gather(x, col).reshape(total, -1)
             return gather(x, col, cols, send_col).reshape(total, -1)
 
         def all_scatter(x):

time: 230 us -> 217 us (0.943)
  waiting for transfers between devices: 83.2 us -> 60.5 us
  local copies, waits for them, and re-layouts: 5.16 us -> 10.9 us
  matrix products: 13.3 us -> 17.7 us
  starting transfers between devices: 122 us -> 119 us
  other arithmetic: 2.86 us -> 5.85 us
    ppermute x36, waiting for transfers between devices: 53.9 us -> 37.1 us  [swap_col(): return lax.ppermute(block, 'col', [(i, i ^ bits) for i in range(cols)])]
    ppermute x36, starting transfers between devices: 81.3 us -> 70.8 us  [swap_col(): return lax.ppermute(block, 'col', [(i, i ^ bits) for i in range(cols)])]
    ppermute x24, starting transfers between devices: 33 us -> 39.3 us  [send_group(): lax.ppermute(block, ('layer', 'row'), [(i, (i // pair + step) % groups *...]
    ppermute x24, waiting for transfers between devices: 18.7 us -> 12.5 us  [send_group(): lax.ppermute(block, ('layer', 'row'), [(i, (i // pair + step) % groups *...]
    dynamic_update_slice x33 -> x34, local copies, waits for them, and re-layouts: 0.46 us -> 4.62 us  [place(): out = lax.dynamic_update_index_in_dim(out, block, index, 0)]
    dot_general x2, matrix products: 2.54 us -> 5.91 us  [shards(): jnp.dot(col_gather(forward.astype(BF16)), lower_coupling[0], preferred_el...]
    dynamic_update_slice x10, other arithmetic: 0.98 us -> 3.89 us  [place(): out = lax.dynamic_update_index_in_dim(out, block, index, 0)]
  transfers between devices with their start and end apart: 76 -> 76, of which waited for: 30 -> 36; matrix products, arithmetic and copies ran while one was open for 8% -> 14% of each run, Pallas kernels for 0% -> 0%
where the time goes in v2:
time: 217 us
  starting transfers between devices  119 us (55%)
  waiting for transfers between devices  60.5 us (28%)
  matrix products  17.7 us (8%)
  local copies, waits for them, and re-layouts  10.9 us (5%)
  other arithmetic  5.85 us (3%)
  between operations  2.73 us (1%)
    ppermute x36, starting transfers between devices, swap_col(): return lax.ppermute(block, 'col', [(i, i ^ bits) for i in range(cols)])  70.8 us
    ppermute x24, starting transfers between devices, send_group(): lax.ppermute(block, ('layer', 'row'), [(i, (i // pair + step) % groups *...  39.3 us
    ppermute x36, waiting for transfers between devices, swap_col(): return lax.ppermute(block, 'col', [(i, i ^ bits) for i in range(cols)])  37.1 us
    ppermute x24, waiting for transfers between devices, send_group(): lax.ppermute(block, ('layer', 'row'), [(i, (i // pair + step) % groups *...  12.5 us
    dot_general x10, matrix products, dot_nt(): lax.dot_general(a, b, (((1,), (1,)), ((), ())), preferred_element_type=F32)  11.8 us
    ppermute x4, waiting for transfers between devices, send_high(): lax.ppermute(block, 'row', [(i, (i // pair + step) % high * pair + i % pa...  10.7 us
    ppermute x4, starting transfers between devices, send_high(): lax.ppermute(block, 'row', [(i, (i // pair + step) % high * pair + i % pa...  6.95 us
    dot_general x2, matrix products, shards(): jnp.dot(col_gather(forward.astype(BF16)), lower_coupling[0], preferred_el...  5.91 us
  transfers between devices with their start and end apart: 76, of which 36 were waited for; matrix products, arithmetic and copies ran while one was open for 14% of the time, Pallas kernels for 0%

profile of v2, /device:TPU:0, one launch (start us, length us, event | category | flops | bytes accessed | tf_op | source)
XLA Modules:
  0.0 217.0 jit_solution(8021397173103896000)
XLA Ops:
  2.8 3.0 %collective-permute-start.38 = (bf16[64,1024]{1,0:T(8,128)(2,1)S(1)}, bf16[64,1024]{1,0:T(8,128)(2,1)S(1)}, u32[]{:S(2)}, u32[]{:S(2)}) collective-permute-start(bf16[64,1024]{1,0:T(8,128)(2,1)S(1)} %bitcast.444), channel_id=1, source_target_pairs={{0,8},{4,12},{8,0},{12,4},{1,9},{5,13},{9,1},{13,5},{2,10},{6,14},... | collective-permute-start | bytes 393224 | tf_op jit(solution)/shard_map/ppermute | solution.py:35
  6.1 4.1 %collective-permute-done.38 = bf16[64,1024]{1,0:T(8,128)(2,1)S(1)} collective-permute-done((bf16[64,1024]{1,0:T(8,128)(2,1)S(1)}, bf16[64,1024]{1,0:T(8,128)(2,1)S(1)}, u32[]{:S(2)}, u32[]{:S(2)}) %collective-permute-start.38) | collective-permute-done | bytes 131104 | tf_op jit(solution)/shard_map/ppermute | solution.py:35
  19.6 3.7 %collective-permute-start.42 = (bf16[64,1024]{1,0:T(8,128)(2,1)S(1)}, bf16[64,1024]{1,0:T(8,128)(2,1)S(1)}, u32[]{:S(2)}, u32[]{:S(2)}) collective-permute-start(bf16[64,1024]{1,0:T(8,128)(2,1)S(1)} %fusion.46), channel_id=1, source_target_pairs={{0,3},{1,2},{2,1},{3,0},{4,7},{5,6},{6,5},{7,4},{8,11},{9,10},{10,... | collective-permute-start | bytes 393224 | tf_op jit(solution)/shard_map/ppermute | solution.py:68
  25.2 3.7 %collective-permute-start.4 = (bf16[64,1024]{1,0:T(8,128)(2,1)S(1)}, bf16[64,1024]{1,0:T(8,128)(2,1)S(1)}, u32[]{:S(2)}, u32[]{:S(2)}) collective-permute-start(bf16[64,1024]{1,0:T(8,128)(2,1)S(1)} %fusion.62), channel_id=1, source_target_pairs={{0,3},{1,2},{2,1},{3,0},{4,7},{5,6},{6,5},{7,4},{8,11},{9,10},{10,... | collective-permute-start | bytes 393224 | tf_op jit(solution)/shard_map/ppermute | solution.py:68
  29.0 4.0 %collective-permute-done.42 = bf16[64,1024]{1,0:T(8,128)(2,1)S(1)} collective-permute-done((bf16[64,1024]{1,0:T(8,128)(2,1)S(1)}, bf16[64,1024]{1,0:T(8,128)(2,1)S(1)}, u32[]{:S(2)}, u32[]{:S(2)}) %collective-permute-start.42) | collective-permute-done | bytes 131104 | tf_op jit(solution)/shard_map/ppermute | solution.py:68
  37.3 8.0 %collective-permute-start.43 = (bf16[64,1024]{1,0:T(8,128)(2,1)S(1)}, bf16[64,1024]{1,0:T(8,128)(2,1)S(1)}, u32[]{:S(2)}, u32[]{:S(2)}) collective-permute-start(bf16[64,1024]{1,0:T(8,128)(2,1)S(1)} %get-tuple-element.33), channel_id=1, source_target_pairs={{0,1},{1,0},{2,3},{3,2},{4,5},{5,4},{6,7},{7,6},{8,9},{9,8},{10,11... | collective-permute-start | bytes 393224 | tf_op jit(solution)/shard_map/ppermute | solution.py:68
  52.7 3.6 %fusion.4 = f32[4,2,32,2048]{3,2,1,0:T(8,128)S(1)} fusion(bf16[4,2,32,1024]{3,2,1,0:T(8,128)(2,1)S(1)} %bitcast.429, bf16[1,1024,2048]{2,1,0:T(8,128)(2,1)} %param.11), kind=kOutput, calls=%fused_computation.4 | convolution fusion | flops 1073741824 | bytes 6815744 | tf_op jit(solution)/shard_map/dot_general | solution.py:157
  60.5 3.7 %collective-permute-start.47 = (bf16[32,2048]{1,0:T(8,128)(2,1)S(1)}, bf16[32,2048]{1,0:T(8,128)(2,1)S(1)}, u32[]{:S(2)}, u32[]{:S(2)}) collective-permute-start(bf16[32,2048]{1,0:T(8,128)(2,1)S(1)} %get-tuple-element.53), channel_id=1, source_target_pairs={{0,8},{4,12},{8,16},{12,20},{16,24},{20,28},{24,0},{28,4},{1,9},{5... | collective-permute-start | bytes 393224 | tf_op jit(solution)/shard_map/ppermute | solution.py:45
  71.1 4.0 %collective-permute-start.50 = (bf16[32,2048]{1,0:T(8,128)(2,1)S(1)}, bf16[32,2048]{1,0:T(8,128)(2,1)S(1)}, u32[]{:S(2)}, u32[]{:S(2)}) collective-permute-start(bf16[32,2048]{1,0:T(8,128)(2,1)S(1)} %get-tuple-element.29), channel_id=1, source_target_pairs={{0,8},{4,12},{8,16},{12,20},{16,24},{20,28},{24,0},{28,4},{1,9},{5... | collective-permute-start | bytes 393224 | tf_op jit(solution)/shard_map/ppermute | solution.py:45
  76.8 3.9 %collective-permute-start.12 = (bf16[32,2048]{1,0:T(8,128)(2,1)S(1)}, bf16[32,2048]{1,0:T(8,128)(2,1)S(1)}, u32[]{:S(2)}, u32[]{:S(2)}) collective-permute-start(bf16[32,2048]{1,0:T(8,128)(2,1)S(1)} %get-tuple-element.14), channel_id=1, source_target_pairs={{0,8},{4,12},{8,16},{12,20},{16,24},{20,28},{24,0},{28,4},{1,9},{5... | collective-permute-start | bytes 393224 | tf_op jit(solution)/shard_map/ppermute | solution.py:45
  81.7 2.8 %collective-permute-start.14 = (bf16[32,2048]{1,0:T(8,128)(2,1)S(1)}, bf16[32,2048]{1,0:T(8,128)(2,1)S(1)}, u32[]{:S(2)}, u32[]{:S(2)}) collective-permute-start(bf16[32,2048]{1,0:T(8,128)(2,1)S(1)} %get-tuple-element.14), channel_id=1, source_target_pairs={{0,24},{4,28},{8,0},{12,4},{16,8},{20,12},{24,16},{28,20},{1,25},{... | collective-permute-start | bytes 393224 | tf_op jit(solution)/shard_map/ppermute | solution.py:45
  97.6 3.7 %collective-permute-done.17 = bf16[64,1024]{1,0:T(8,128)(2,1)S(1)} collective-permute-done((bf16[64,1024]{1,0:T(8,128)(2,1)S(1)}, bf16[64,1024]{1,0:T(8,128)(2,1)S(1)}, u32[]{:S(2)}, u32[]{:S(2)}) %collective-permute-start.17) | collective-permute-done | bytes 131104 | tf_op jit(solution)/shard_map/ppermute | solution.py:68
  103.2 5.3 %collective-permute-done.56 = bf16[64,1024]{1,0:T(8,128)(2,1)S(1)} collective-permute-done((bf16[64,1024]{1,0:T(8,128)(2,1)S(1)}, bf16[64,1024]{1,0:T(8,128)(2,1)S(1)}, u32[]{:S(2)}, u32[]{:S(2)}) %collective-permute-start.56) | collective-permute-done | bytes 131104 | tf_op jit(solution)/shard_map/ppermute | solution.py:68
  113.1 8.1 %collective-permute-start.57 = (bf16[64,1024]{1,0:T(8,128)(2,1)S(1)}, bf16[64,1024]{1,0:T(8,128)(2,1)S(1)}, u32[]{:S(2)}, u32[]{:S(2)}) collective-permute-start(bf16[64,1024]{1,0:T(8,128)(2,1)S(1)} %get-tuple-element.27), channel_id=1, source_target_pairs={{0,1},{1,0},{2,3},{3,2},{4,5},{5,4},{6,7},{7,6},{8,9},{9,8},{10,11... | collective-permute-start | bytes 393224 | tf_op jit(solution)/shard_map/ppermute | solution.py:68
  132.5 3.8 %collective-permute-start.61 = (bf16[32,2048]{1,0:T(8,128)(2,1)S(1)}, bf16[32,2048]{1,0:T(8,128)(2,1)S(1)}, u32[]{:S(2)}, u32[]{:S(2)}) collective-permute-start(bf16[32,2048]{1,0:T(8,128)(2,1)S(1)} %get-tuple-element.48), channel_id=1, source_target_pairs={{0,8},{4,12},{8,16},{12,20},{16,24},{20,28},{24,0},{28,4},{1,9},{5... | collective-permute-start | bytes 393224 | tf_op jit(solution)/shard_map/ppermute | solution.py:45
  144.2 2.8 %collective-permute-start.64 = (bf16[32,2048]{1,0:T(8,128)(2,1)S(1)}, bf16[32,2048]{1,0:T(8,128)(2,1)S(1)}, u32[]{:S(2)}, u32[]{:S(2)}) collective-permute-start(bf16[32,2048]{1,0:T(8,128)(2,1)S(1)} %get-tuple-element.22), channel_id=1, source_target_pairs={{0,8},{4,12},{8,16},{12,20},{16,24},{20,28},{24,0},{28,4},{1,9},{5... | collective-permute-start | bytes 393224 | tf_op jit(solution)/shard_map/ppermute | solution.py:45
  147.7 2.8 %collective-permute-start.66 = (bf16[32,2048]{1,0:T(8,128)(2,1)S(1)}, bf16[32,2048]{1,0:T(8,128)(2,1)S(1)}, u32[]{:S(2)}, u32[]{:S(2)}) collective-permute-start(bf16[32,2048]{1,0:T(8,128)(2,1)S(1)} %get-tuple-element.22), channel_id=1, source_target_pairs={{0,24},{4,28},{8,0},{12,4},{16,8},{20,12},{24,16},{28,20},{1,25},{... | collective-permute-start | bytes 393224 | tf_op jit(solution)/shard_map/ppermute | solution.py:45
  167.8 2.6 %collective-permute-start.70 = (bf16[64,1024]{1,0:T(8,128)(2,1)S(1)}, bf16[64,1024]{1,0:T(8,128)(2,1)S(1)}, u32[]{:S(2)}, u32[]{:S(2)}) collective-permute-start(bf16[64,1024]{1,0:T(8,128)(2,1)S(1)} %fusion.34), channel_id=1, source_target_pairs={{0,3},{1,2},{2,1},{3,0},{4,7},{5,6},{6,5},{7,4},{8,11},{9,10},{10,... | collective-permute-start | bytes 393224 | tf_op jit(solution)/shard_map/ppermute | solution.py:68
  170.4 3.0 %collective-permute-done.31 = bf16[64,1024]{1,0:T(8,128)(2,1)S(1)} collective-permute-done((bf16[64,1024]{1,0:T(8,128)(2,1)S(1)}, bf16[64,1024]{1,0:T(8,128)(2,1)S(1)}, u32[]{:S(2)}, u32[]{:S(2)}) %collective-permute-start.31) | collective-permute-done | bytes 131104 | tf_op jit(solution)/shard_map/ppermute | solution.py:68
  173.4 2.6 %collective-permute-start.32 = (bf16[64,1024]{1,0:T(8,128)(2,1)S(1)}, bf16[64,1024]{1,0:T(8,128)(2,1)S(1)}, u32[]{:S(2)}, u32[]{:S(2)}) collective-permute-start(bf16[64,1024]{1,0:T(8,128)(2,1)S(1)} %fusion.50), channel_id=1, source_target_pairs={{0,3},{1,2},{2,1},{3,0},{4,7},{5,6},{6,5},{7,4},{8,11},{9,10},{10,... | collective-permute-start | bytes 393224 | tf_op jit(solution)/shard_map/ppermute | solution.py:68
  176.0 5.3 %collective-permute-done.70 = bf16[64,1024]{1,0:T(8,128)(2,1)S(1)} collective-permute-done((bf16[64,1024]{1,0:T(8,128)(2,1)S(1)}, bf16[64,1024]{1,0:T(8,128)(2,1)S(1)}, u32[]{:S(2)}, u32[]{:S(2)}) %collective-permute-start.70) | collective-permute-done | bytes 131104 | tf_op jit(solution)/shard_map/ppermute | solution.py:68
  186.2 2.6 %collective-permute-start.34 = (bf16[64,1024]{1,0:T(8,128)(2,1)}, bf16[64,1024]{1,0:T(8,128)(2,1)S(1)}, u32[]{:S(2)}, u32[]{:S(2)}) collective-permute-start(bf16[64,1024]{1,0:T(8,128)(2,1)} %get-tuple-element.5), channel_id=1, source_target_pairs={{0,3},{1,2},{2,1},{3,0},{4,7},{5,6},{6,5},{7,4},{8,11},{9,10},{10,... | collective-permute-start | bytes 393224 | tf_op jit(solution)/shard_map/ppermute | solution.py:68
  206.3 2.9 %collective-permute-start.75 = (bf16[64,1024]{1,0:T(8,128)(2,1)S(1)}, bf16[64,1024]{1,0:T(8,128)(2,1)S(1)}, u32[]{:S(2)}, u32[]{:S(2)}) collective-permute-start(bf16[64,1024]{1,0:T(8,128)(2,1)S(1)} %fusion.66), channel_id=1, source_target_pairs={{0,8},{4,12},{8,0},{12,4},{1,9},{5,13},{9,1},{13,5},{2,10},{6,14},... | collective-permute-start | bytes 393224 | tf_op jit(solution)/shard_map/ppermute | solution.py:35
  211.1 2.4 %collective-permute-done.75 = bf16[64,1024]{1,0:T(8,128)(2,1)S(1)} collective-permute-done((bf16[64,1024]{1,0:T(8,128)(2,1)S(1)}, bf16[64,1024]{1,0:T(8,128)(2,1)S(1)}, u32[]{:S(2)}, u32[]{:S(2)}) %collective-permute-start.75) | collective-permute-done | bytes 131104 | tf_op jit(solution)/shard_map/ppermute | solution.py:35
  (294 shorter events, 121.7 us)
Async XLA Ops:
  15.1 13.9 %collective-permute-start.40 = (bf16[64,1024]{1,0:T(8,128)(2,1)S(1)}, bf16[64,1024]{1,0:T(8,128)(2,1)S(1)}, u32[]{:S(2)}, u32[]{:S(2)}) collective-permute-start(bf16[64,1024]{1,0:T(8,128)(2,1)S(1)} %get-tuple-element.56), channel_id=1, source_target_pairs={{0,1},{1,0},{2,3},{3,2},{4,5},{5,4},{6,7},{7,6},{8,9},{9,8},{10,11... | collective-permute-start | bytes 393224 | tf_op jit(solution)/shard_map/ppermute | solution.py:68
  18.0 16.7 %collective-permute-start.2 = (bf16[64,1024]{1,0:T(8,128)(2,1)S(1)}, bf16[64,1024]{1,0:T(8,128)(2,1)S(1)}, u32[]{:S(2)}, u32[]{:S(2)}) collective-permute-start(bf16[64,1024]{1,0:T(8,128)(2,1)S(1)} %get-tuple-element.44), channel_id=1, source_target_pairs={{0,1},{1,0},{2,3},{3,2},{4,5},{5,4},{6,7},{7,6},{8,9},{9,8},{10,11... | collective-permute-start | bytes 393224 | tf_op jit(solution)/shard_map/ppermute | solution.py:68
  19.6 13.4 %collective-permute-start.42 = (bf16[64,1024]{1,0:T(8,128)(2,1)S(1)}, bf16[64,1024]{1,0:T(8,128)(2,1)S(1)}, u32[]{:S(2)}, u32[]{:S(2)}) collective-permute-start(bf16[64,1024]{1,0:T(8,128)(2,1)S(1)} %fusion.46), channel_id=1, source_target_pairs={{0,3},{1,2},{2,1},{3,0},{4,7},{5,6},{6,5},{7,4},{8,11},{9,10},{10,... | collective-permute-start | bytes 393224 | tf_op jit(solution)/shard_map/ppermute | solution.py:68
  25.2 10.2 %collective-permute-start.4 = (bf16[64,1024]{1,0:T(8,128)(2,1)S(1)}, bf16[64,1024]{1,0:T(8,128)(2,1)S(1)}, u32[]{:S(2)}, u32[]{:S(2)}) collective-permute-start(bf16[64,1024]{1,0:T(8,128)(2,1)S(1)} %fusion.62), channel_id=1, source_target_pairs={{0,3},{1,2},{2,1},{3,0},{4,7},{5,6},{6,5},{7,4},{8,11},{9,10},{10,... | collective-permute-start | bytes 393224 | tf_op jit(solution)/shard_map/ppermute | solution.py:68
  33.2 12.2 %collective-permute-start.44 = (bf16[64,1024]{1,0:T(8,128)(2,1)S(1)}, bf16[64,1024]{1,0:T(8,128)(2,1)S(1)}, u32[]{:S(2)}, u32[]{:S(2)}) collective-permute-start(bf16[64,1024]{1,0:T(8,128)(2,1)S(1)} %get-tuple-element.33), channel_id=1, source_target_pairs={{0,3},{1,2},{2,1},{3,0},{4,7},{5,6},{6,5},{7,4},{8,11},{9,10},{10,... | collective-permute-start | bytes 393224 | tf_op jit(solution)/shard_map/ppermute | solution.py:68
  35.6 11.7 %collective-permute-start.6 = (bf16[64,1024]{1,0:T(8,128)(2,1)S(1)}, bf16[64,1024]{1,0:T(8,128)(2,1)S(1)}, u32[]{:S(2)}, u32[]{:S(2)}) collective-permute-start(bf16[64,1024]{1,0:T(8,128)(2,1)S(1)} %get-tuple-element.18), channel_id=1, source_target_pairs={{0,3},{1,2},{2,1},{3,0},{4,7},{5,6},{6,5},{7,4},{8,11},{9,10},{10,... | collective-permute-start | bytes 393224 | tf_op jit(solution)/shard_map/ppermute | solution.py:68
  37.3 12.2 %collective-permute-start.43 = (bf16[64,1024]{1,0:T(8,128)(2,1)S(1)}, bf16[64,1024]{1,0:T(8,128)(2,1)S(1)}, u32[]{:S(2)}, u32[]{:S(2)}) collective-permute-start(bf16[64,1024]{1,0:T(8,128)(2,1)S(1)} %get-tuple-element.33), channel_id=1, source_target_pairs={{0,1},{1,0},{2,3},{3,2},{4,5},{5,4},{6,7},{7,6},{8,9},{9,8},{10,11... | collective-permute-start | bytes 393224 | tf_op jit(solution)/shard_map/ppermute | solution.py:68
  66.0 10.3 %collective-permute-start.10 = (bf16[32,2048]{1,0:T(8,128)(2,1)S(1)}, bf16[32,2048]{1,0:T(8,128)(2,1)S(1)}, u32[]{:S(2)}, u32[]{:S(2)}) collective-permute-start(bf16[32,2048]{1,0:T(8,128)(2,1)S(1)} %get-tuple-element.43), channel_id=1, source_target_pairs={{0,16},{4,20},{8,24},{12,28},{16,0},{20,4},{24,8},{28,12},{1,17},{... | collective-permute-start | bytes 393224 | tf_op jit(solution)/shard_map/ppermute | solution.py:45
  66.6 10.1 %collective-permute-start.11 = (bf16[32,2048]{1,0:T(8,128)(2,1)S(1)}, bf16[32,2048]{1,0:T(8,128)(2,1)S(1)}, u32[]{:S(2)}, u32[]{:S(2)}) collective-permute-start(bf16[32,2048]{1,0:T(8,128)(2,1)S(1)} %get-tuple-element.42), channel_id=1, source_target_pairs={{0,24},{4,28},{8,0},{12,4},{16,8},{20,12},{24,16},{28,20},{1,25},{... | collective-permute-start | bytes 393224 | tf_op jit(solution)/shard_map/ppermute | solution.py:45
  71.1 10.6 %collective-permute-start.50 = (bf16[32,2048]{1,0:T(8,128)(2,1)S(1)}, bf16[32,2048]{1,0:T(8,128)(2,1)S(1)}, u32[]{:S(2)}, u32[]{:S(2)}) collective-permute-start(bf16[32,2048]{1,0:T(8,128)(2,1)S(1)} %get-tuple-element.29), channel_id=1, source_target_pairs={{0,8},{4,12},{8,16},{12,20},{16,24},{20,28},{24,0},{28,4},{1,9},{5... | collective-permute-start | bytes 393224 | tf_op jit(solution)/shard_map/ppermute | solution.py:45
  91.1 12.2 %collective-permute-start.54 = (bf16[64,1024]{1,0:T(8,128)(2,1)S(1)}, bf16[64,1024]{1,0:T(8,128)(2,1)S(1)}, u32[]{:S(2)}, u32[]{:S(2)}) collective-permute-start(bf16[64,1024]{1,0:T(8,128)(2,1)S(1)} %get-tuple-element.51), channel_id=1, source_target_pairs={{0,1},{1,0},{2,3},{3,2},{4,5},{5,4},{6,7},{7,6},{8,9},{9,8},{10,11... | collective-permute-start | bytes 393224 | tf_op jit(solution)/shard_map/ppermute | solution.py:68
  94.5 16.1 %collective-permute-start.16 = (bf16[64,1024]{1,0:T(8,128)(2,1)S(1)}, bf16[64,1024]{1,0:T(8,128)(2,1)S(1)}, u32[]{:S(2)}, u32[]{:S(2)}) collective-permute-start(bf16[64,1024]{1,0:T(8,128)(2,1)S(1)} %get-tuple-element.39), channel_id=1, source_target_pairs={{0,1},{1,0},{2,3},{3,2},{4,5},{5,4},{6,7},{7,6},{8,9},{9,8},{10,11... | collective-permute-start | bytes 393224 | tf_op jit(solution)/shard_map/ppermute | solution.py:68
  95.7 12.9 %collective-permute-start.56 = (bf16[64,1024]{1,0:T(8,128)(2,1)S(1)}, bf16[64,1024]{1,0:T(8,128)(2,1)S(1)}, u32[]{:S(2)}, u32[]{:S(2)}) collective-permute-start(bf16[64,1024]{1,0:T(8,128)(2,1)S(1)} %fusion.41), channel_id=1, source_target_pairs={{0,3},{1,2},{2,1},{3,0},{4,7},{5,6},{6,5},{7,4},{8,11},{9,10},{10,... | collective-permute-start | bytes 393224 | tf_op jit(solution)/shard_map/ppermute | solution.py:68
  108.7 12.6 %collective-permute-start.58 = (bf16[64,1024]{1,0:T(8,128)(2,1)S(1)}, bf16[64,1024]{1,0:T(8,128)(2,1)S(1)}, u32[]{:S(2)}, u32[]{:S(2)}) collective-permute-start(bf16[64,1024]{1,0:T(8,128)(2,1)S(1)} %get-tuple-element.27), channel_id=1, source_target_pairs={{0,3},{1,2},{2,1},{3,0},{4,7},{5,6},{6,5},{7,4},{8,11},{9,10},{10,... | collective-permute-start | bytes 393224 | tf_op jit(solution)/shard_map/ppermute | solution.py:68
  111.1 12.2 %collective-permute-start.20 = (bf16[64,1024]{1,0:T(8,128)(2,1)S(1)}, bf16[64,1024]{1,0:T(8,128)(2,1)S(1)}, u32[]{:S(2)}, u32[]{:S(2)}) collective-permute-start(bf16[64,1024]{1,0:T(8,128)(2,1)S(1)} %get-tuple-element.12), channel_id=1, source_target_pairs={{0,3},{1,2},{2,1},{3,0},{4,7},{5,6},{6,5},{7,4},{8,11},{9,10},{10,... | collective-permute-start | bytes 393224 | tf_op jit(solution)/shard_map/ppermute | solution.py:68
  113.1 12.2 %collective-permute-start.57 = (bf16[64,1024]{1,0:T(8,128)(2,1)S(1)}, bf16[64,1024]{1,0:T(8,128)(2,1)S(1)}, u32[]{:S(2)}, u32[]{:S(2)}) collective-permute-start(bf16[64,1024]{1,0:T(8,128)(2,1)S(1)} %get-tuple-element.27), channel_id=1, source_target_pairs={{0,1},{1,0},{2,3},{3,2},{4,5},{5,4},{6,7},{7,6},{8,9},{9,8},{10,11... | collective-permute-start | bytes 393224 | tf_op jit(solution)/shard_map/ppermute | solution.py:68
  138.5 12.1 %collective-permute-start.24 = (bf16[32,2048]{1,0:T(8,128)(2,1)S(1)}, bf16[32,2048]{1,0:T(8,128)(2,1)S(1)}, u32[]{:S(2)}, u32[]{:S(2)}) collective-permute-start(bf16[32,2048]{1,0:T(8,128)(2,1)S(1)} %get-tuple-element.38), channel_id=1, source_target_pairs={{0,16},{4,20},{8,24},{12,28},{16,0},{20,4},{24,8},{28,12},{1,17},{... | collective-permute-start | bytes 393224 | tf_op jit(solution)/shard_map/ppermute | solution.py:45
  163.1 12.9 %collective-permute-start.68 = (bf16[64,1024]{1,0:T(8,128)(2,1)S(1)}, bf16[64,1024]{1,0:T(8,128)(2,1)S(1)}, u32[]{:S(2)}, u32[]{:S(2)}) collective-permute-start(bf16[64,1024]{1,0:T(8,128)(2,1)S(1)} %get-tuple-element.46), channel_id=1, source_target_pairs={{0,1},{1,0},{2,3},{3,2},{4,5},{5,4},{6,7},{7,6},{8,9},{9,8},{10,11... | collective-permute-start | bytes 393224 | tf_op jit(solution)/shard_map/ppermute | solution.py:68
  166.6 17.9 %collective-permute-start.30 = (bf16[64,1024]{1,0:T(8,128)(2,1)S(1)}, bf16[64,1024]{1,0:T(8,128)(2,1)S(1)}, u32[]{:S(2)}, u32[]{:S(2)}) collective-permute-start(bf16[64,1024]{1,0:T(8,128)(2,1)S(1)} %get-tuple-element.34), channel_id=1, source_target_pairs={{0,1},{1,0},{2,3},{3,2},{4,5},{5,4},{6,7},{7,6},{8,9},{9,8},{10,11... | collective-permute-start | bytes 393224 | tf_op jit(solution)/shard_map/ppermute | solution.py:68
  167.8 13.5 %collective-permute-start.70 = (bf16[64,1024]{1,0:T(8,128)(2,1)S(1)}, bf16[64,1024]{1,0:T(8,128)(2,1)S(1)}, u32[]{:S(2)}, u32[]{:S(2)}) collective-permute-start(bf16[64,1024]{1,0:T(8,128)(2,1)S(1)} %fusion.34), channel_id=1, source_target_pairs={{0,3},{1,2},{2,1},{3,0},{4,7},{5,6},{6,5},{7,4},{8,11},{9,10},{10,... | collective-permute-start | bytes 393224 | tf_op jit(solution)/shard_map/ppermute | solution.py:68
  173.4 11.1 %collective-permute-start.32 = (bf16[64,1024]{1,0:T(8,128)(2,1)S(1)}, bf16[64,1024]{1,0:T(8,128)(2,1)S(1)}, u32[]{:S(2)}, u32[]{:S(2)}) collective-permute-start(bf16[64,1024]{1,0:T(8,128)(2,1)S(1)} %fusion.50), channel_id=1, source_target_pairs={{0,3},{1,2},{2,1},{3,0},{4,7},{5,6},{6,5},{7,4},{8,11},{9,10},{10,... | collective-permute-start | bytes 393224 | tf_op jit(solution)/shard_map/ppermute | solution.py:68
  189.2 10.1 %collective-permute-start.33 = (bf16[64,1024]{1,0:T(8,128)(2,1)}, bf16[64,1024]{1,0:T(8,128)(2,1)S(1)}, u32[]{:S(2)}, u32[]{:S(2)}) collective-permute-start(bf16[64,1024]{1,0:T(8,128)(2,1)} %get-tuple-element.5), channel_id=1, source_target_pairs={{0,1},{1,0},{2,3},{3,2},{4,5},{5,4},{6,7},{7,6},{8,9},{9,8},{10,11... | collective-permute-start | bytes 393224 | tf_op jit(solution)/shard_map/ppermute | solution.py:68
  190.9 11.1 %collective-permute-start.73 = (bf16[64,1024]{1,0:T(8,128)(2,1)}, bf16[64,1024]{1,0:T(8,128)(2,1)S(1)}, u32[]{:S(2)}, u32[]{:S(2)}) collective-permute-start(bf16[64,1024]{1,0:T(8,128)(2,1)} %collective-permute-done.72), channel_id=1, source_target_pairs={{0,1},{1,0},{2,3},{3,2},{4,5},{5,4},{6,7},{7,6},{8,9},{9,8},{10,11... | collective-permute-start | bytes 393224 | tf_op jit(solution)/shard_map/ppermute | solution.py:68
  194.6 10.1 %collective-permute-start.35 = (bf16[64,1024]{1,0:T(8,128)(2,1)S(1)}, bf16[64,1024]{1,0:T(8,128)(2,1)S(1)}, u32[]{:S(2)}, u32[]{:S(2)}) collective-permute-start(bf16[64,1024]{1,0:T(8,128)(2,1)S(1)} %collective-permute-done.34), channel_id=1, source_target_pairs={{0,1},{1,0},{2,3},{3,2},{4,5},{5,4},{6,7},{7,6},{8,9},{9,8},{10,11... | collective-permute-start | bytes 393224 | tf_op jit(solution)/shard_map/ppermute | solution.py:68
  (72 other events, 546.2 us)

commit v3 on v1

--- a/solution.py
+++ b/solution.py
@@ -16,6 +16,52 @@
     for index, block in parts:
         out = lax.dynamic_update_index_in_dim(out, block, index, 0)
     return out
+
+
+WAITS = (1, None, None, None)
+
+
+def alone(steps):
+    try:
+        event = next(steps)
+        while True:
+            event = steps.send(None)
+    except StopIteration as end:
+        return end.value
+
+
+def staggered(first, second):
+    ends = {}
+    events = {}
+
+    def step(name, chunk, wait=None):
+        try:
+            events[name] = chunk.send(wait) if name in events else next(chunk)
+        except StopIteration as end:
+            ends[name] = end.value
+            return None
+        return events[name]
+
+    step("a", first)
+    step("b", second)
+    last = None
+    for _ in range(4):
+        last = step("a", first)
+    ahead, behind = ("b", second), ("a", first)
+    for stage in range(5):
+        seen = [last]
+        for wait in WAITS:
+            while wait is not None and len(seen) <= wait:
+                seen.append(None if behind[0] in ends else step(*behind))
+            got = step(*ahead, None if wait is None else seen[wait])
+        last = got
+        while len(seen) < 6:
+            seen.append(None if behind[0] in ends else step(*behind))
+        ahead, behind = behind, ahead
+    for name, chunk in (("a", first), ("b", second)):
+        while name not in ends:
+            step(name, chunk)
+    return ends["a"], ends["b"]
 
 
 def dot_nt(a, b):
@@ -60,23 +106,53 @@
         return total
 
     def gather(block, me, size, send):
-        return place(
-            [(me, block)] + [((me - k) % size, send(block, k)) for k in range(1, size)]
-        )
+        parts = [(me, block)]
+        parts += [((me - k) % size, send(block, k)) for k in range(1, size)]
+        return place(parts), parts[-1][1]
+
+    def swap_col(block, bits):
+        return lax.ppermute(block, "col", [(i, i ^ bits) for i in range(cols)])
+
+    def after(block, event):
+        if event is None:
+            return block
+        row = event.reshape(-1, event.shape[-1])[:1, : block.shape[-1]].astype(F32)
+        return block + jnp.where((row < 0) & (row > 0), row, 0).astype(block.dtype)
+
+    def line_scatter(part, me, event):
+        low = part.astype(BF16)
+        far = swap_col(after(pick(low, me ^ 2), event), 1)
+        near = swap_col(after(pick(low, me ^ 1), event), 1)
+        event = yield far
+        across = pick(part, me ^ 3) + far.astype(F32)
+        across = swap_col(after(across, event).astype(BF16), 3)
+        event = yield across
+        return pick(part, me) + near.astype(F32) + across.astype(F32), event
+
+    def line_gather(block, me, event):
+        block = after(block, event)
+        across = swap_col(block, 3)
+        near = swap_col(block, 1)
+        event = yield across
+        far = swap_col(after(across, event), 1)
+        event = yield far
+        return place([(me, block), (me ^ 1, near), (me ^ 3, across), (me ^ 2, far)]), event
 
     def pair_scatter(part, core):
         if pair == 1:
-            return part[:, 0]
+            return part[:, 0], part
         mine = lax.dynamic_index_in_dim(part, core, 1, keepdims=False)
         other = lax.dynamic_index_in_dim(part, 1 - core, 1, keepdims=False)
-        return mine + send_pair(other.astype(BF16)).astype(F32)
+        got = send_pair(other.astype(BF16))
+        return mine + got.astype(F32), got
 
     def pair_gather(block, core):
         if pair == 1:
-            return block[:, None]
+            return block[:, None], block
+        got = send_pair(block)
         out = jnp.zeros((block.shape[0], pair) + block.shape[1:], block.dtype)
         out = lax.dynamic_update_index_in_dim(out, block, core, 1)
-        return lax.dynamic_update_index_in_dim(out, send_pair(block), 1 - core, 1)
+        return lax.dynamic_update_index_in_dim(out, got, 1 - core, 1), got
 
     def shards(
         lower_inverse,
@@ -102,52 +178,75 @@
         col_mask = (col * col_count + lax.iota(jnp.int32, col_count) < limit).astype(F32)
         row_mask = (row * row_count + lax.iota(jnp.int32, row_count) < limit).astype(F32)
 
-        def col_scatter(x):
-            return scatter(x.reshape(cols, -1, x.shape[1]), col, cols, send_col)
-
-        def col_gather(x):
-            return gather(x, col, cols, send_col).reshape(total, -1)
+        def col_scatter(x, event):
+            pieces = x.reshape(cols, -1, x.shape[1])
+            if cols == 4:
+                return (yield from line_scatter(pieces, col, event))
+            return scatter(pieces, col, cols, send_col), None
+
+        def col_gather(x, event):
+            if cols == 4:
+                out, event = yield from line_gather(x, col, event)
+            else:
+                out = gather(x, col, cols, send_col)[0]
+            return out.reshape(total, -1), event
 
         def all_scatter(x):
             n = x.shape[1]
-            mine = pair_scatter(x.reshape(groups, pair, part, n), core)
-            return scatter(mine, group, groups, send_group)
+            mine, got = pair_scatter(x.reshape(groups, pair, part, n), core)
+            yield got
+            out = scatter(mine, group, groups, send_group)
+            yield out
+            return out
 
         def all_gather(x):
-            mine = gather(x, group, groups, send_group)
-            return pair_gather(mine, core).reshape(total, -1)
+            mine, got = gather(x, group, groups, send_group)
+            yield got
+            out, got = pair_gather(mine, core)
+            yield got
+            return out.reshape(total, -1)
 
         def row_gather(x):
-            return pair_gather(gather(x, up, high, send_high), core).reshape(total, -1)
+            mine = gather(x, up, high, send_high)[0]
+            return pair_gather(mine, core)[0].reshape(total, -1)
 
         def row_scatter(x):
             n = x.shape[1]
-            mine = pair_scatter(x.reshape(high, pair, -1, n), core)
+            mine = pair_scatter(x.reshape(high, pair, -1, n), core)[0]
             return scatter(mine, up, high, send_high)
 
         given = (subtree_rhs[0] * col_mask[:, None]).astype(BF16).T
         given = given.reshape(layers, chunks, part, col_count)
         sep_given = separator_rhs.T.reshape(chunks, part, sep_count)
 
-        solved, middles = [], []
-        for h in range(chunks):
+        def chunk(h):
             masked = row_gather(given[:, h].reshape(layers * part, col_count))
-            forward = col_scatter(dot_nt(masked, lower_inverse[0])) * row_mask
-            update = jnp.dot(
-                col_gather(forward.astype(BF16)),
-                lower_coupling[0],
-                preferred_element_type=F32,
+            event = yield None
+            forward, event = yield from col_scatter(dot_nt(masked, lower_inverse[0]), event)
+            forward = lax.optimization_barrier(forward * row_mask)
+            low, _ = yield from col_gather(forward.astype(BF16), event)
+            update = jnp.dot(low, lower_coupling[0], preferred_element_type=F32)
+            share = yield from all_scatter(update)
+            reduced = yield from all_gather((sep_given[h] - share).astype(BF16))
+            event = yield None
+            middle, event = yield from col_scatter(dot_nt(reduced, separator_lower), event)
+            middle, _ = yield from col_gather(middle.astype(BF16), event)
+            spread = yield from all_scatter(dot_nt(middle, separator_upper))
+            got = yield from all_gather(spread.astype(BF16))
+            event = yield None
+            coupled, event = yield from col_scatter(dot_nt(got, upper_coupling[0]), event)
+            interior = ((forward - coupled) * row_mask).astype(BF16)
+            interior, _ = yield from col_gather(interior, event)
+            back = row_scatter(dot_nt(interior, upper_inverse[0])) * col_mask
+            return back.reshape(layers, 1, part, col_count), spread
+
+        solved, middles = zip(
+            *(
+                staggered(chunk(0), chunk(1))
+                if chunks == 2
+                else [alone(chunk(h)) for h in range(chunks)]
             )
-            reduced = all_gather((sep_given[h] - all_scatter(update)).astype(BF16))
-            middle = col_gather(col_scatter(dot_nt(reduced, separator_lower)).astype(BF16))
-            spread = all_scatter(dot_nt(middle, separator_upper))
-            coupled = col_scatter(
-                dot_nt(all_gather(spread.astype(BF16)), upper_coupling[0])
-            )
-            interior = col_gather(((forward - coupled) * row_mask).astype(BF16))
-            back = row_scatter(dot_nt(interior, upper_inverse[0])) * col_mask
-            middles.append(spread)
-            solved.append(back.reshape(layers, 1, part, col_count))
+        )
         out = jnp.concatenate(solved, axis=1).reshape(layers * width, col_count).T
         return out[None], jnp.concatenate(middles, axis=0).T
 

time: 230 us -> 204 us (0.89)
  starting transfers between devices: 122 us -> 88.8 us
  waiting for transfers between devices: 83.2 us -> 89.3 us
    ppermute x36, starting transfers between devices: 81.3 us -> 50.4 us  [swap_col(): return lax.ppermute(block, 'col', [(i, i ^ bits) for i in range(cols)])]
    ppermute x36, waiting for transfers between devices: 53.9 us -> 66.3 us  [swap_col(): return lax.ppermute(block, 'col', [(i, i ^ bits) for i in range(cols)])]
    ppermute x24, waiting for transfers between devices: 18.7 us -> 10.9 us  [send_group(): lax.ppermute(block, ('layer', 'row'), [(i, (i // pair + step) % groups *...]
    ppermute x12, waiting for transfers between devices: 0.19 us -> 2.98 us  [send_pair(): return lax.ppermute(block, 'row', [(i, i ^ 1) for i in range(rows)])]
  transfers between devices with their start and end apart: 76 -> 76, of which waited for: 30 -> 34; matrix products, arithmetic and copies ran while one was open for 8% -> 9% of each run, Pallas kernels for 0% -> 0%
where the time goes in v3:
time: 204 us
  waiting for transfers between devices  89.3 us (44%)
  starting transfers between devices  88.8 us (44%)
  matrix products  13.4 us (7%)
  local copies, waits for them, and re-layouts  7.01 us (3%)
  other arithmetic  2.88 us (1%)
  between operations  2.66 us (1%)
    ppermute x36, waiting for transfers between devices, swap_col(): return lax.ppermute(block, 'col', [(i, i ^ bits) for i in range(cols)])  66.3 us
    ppermute x36, starting transfers between devices, swap_col(): return lax.ppermute(block, 'col', [(i, i ^ bits) for i in range(cols)])  50.4 us
    ppermute x24, starting transfers between devices, send_group(): lax.ppermute(block, ('layer', 'row'), [(i, (i // pair + step) % groups *...  31.8 us
    ppermute x24, waiting for transfers between devices, send_group(): lax.ppermute(block, ('layer', 'row'), [(i, (i // pair + step) % groups *...  10.9 us
    dot_general x10, matrix products, dot_nt(): lax.dot_general(a, b, (((1,), (1,)), ((), ())), preferred_element_type=F32)  10.8 us
    ppermute x4, waiting for transfers between devices, send_high(): lax.ppermute(block, 'row', [(i, (i // pair + step) % high * pair + i % pa...  9.12 us
    ppermute x4, starting transfers between devices, send_high(): lax.ppermute(block, 'row', [(i, (i // pair + step) % high * pair + i % pa...  5.66 us
  transfers between devices with their start and end apart: 76, of which 34 were waited for; matrix products, arithmetic and copies ran while one was open for 9% of the time, Pallas kernels for 0%

profile of v3, /device:TPU:0, one launch (start us, length us, event | category | flops | bytes accessed | tf_op | source)
XLA Modules:
  0.0 204.0 jit_solution(18402552612153423966)
XLA Ops:
  2.8 3.0 %collective-permute-start = (bf16[64,1024]{1,0:T(8,128)(2,1)S(1)}, bf16[64,1024]{1,0:T(8,128)(2,1)S(1)}, u32[]{:S(2)}, u32[]{:S(2)}) collective-permute-start(bf16[64,1024]{1,0:T(8,128)(2,1)S(1)} %bitcast.440), channel_id=1, source_target_pairs={{0,8},{4,12},{8,0},{12,4},{1,9},{5,13},{9,1},{13,5},{2,10},{6,14},... | collective-permute-start | bytes 393224 | tf_op jit(solution)/shard_map/ppermute | solution.py:81
  5.9 3.4 %collective-permute-done = bf16[64,1024]{1,0:T(8,128)(2,1)S(1)} collective-permute-done((bf16[64,1024]{1,0:T(8,128)(2,1)S(1)}, bf16[64,1024]{1,0:T(8,128)(2,1)S(1)}, u32[]{:S(2)}, u32[]{:S(2)}) %collective-permute-start) | collective-permute-done | bytes 131104 | tf_op jit(solution)/shard_map/ppermute | solution.py:81
  15.0 4.4 %collective-permute-done.3 = bf16[64,1024]{1,0:T(8,128)(2,1)S(1)} collective-permute-done((bf16[64,1024]{1,0:T(8,128)(2,1)}, bf16[64,1024]{1,0:T(8,128)(2,1)S(1)}, u32[]{:S(2)}, u32[]{:S(2)}) %collective-permute-start.3) | collective-permute-done | bytes 131104 | tf_op jit(solution)/shard_map/ppermute | solution.py:114
  19.4 3.7 %collective-permute-start.4 = (bf16[64,1024]{1,0:T(8,128)(2,1)S(1)}, bf16[64,1024]{1,0:T(8,128)(2,1)S(1)}, u32[]{:S(2)}, u32[]{:S(2)}) collective-permute-start(bf16[64,1024]{1,0:T(8,128)(2,1)S(1)} %fusion.62), channel_id=1, source_target_pairs={{0,3},{1,2},{2,1},{3,0},{4,7},{5,6},{6,5},{7,4},{8,11},{9,10},{10,... | collective-permute-start | bytes 393224 | tf_op jit(solution)/shard_map/ppermute | solution.py:114
  23.2 3.2 %collective-permute-done.4 = bf16[64,1024]{1,0:T(8,128)(2,1)S(1)} collective-permute-done((bf16[64,1024]{1,0:T(8,128)(2,1)S(1)}, bf16[64,1024]{1,0:T(8,128)(2,1)S(1)}, u32[]{:S(2)}, u32[]{:S(2)}) %collective-permute-start.4) | collective-permute-done | bytes 131104 | tf_op jit(solution)/shard_map/ppermute | solution.py:114
  31.1 4.4 %collective-permute-done.6 = bf16[64,1024]{1,0:T(8,128)(2,1)S(1)} collective-permute-done((bf16[64,1024]{1,0:T(8,128)(2,1)S(1)}, bf16[64,1024]{1,0:T(8,128)(2,1)S(1)}, u32[]{:S(2)}, u32[]{:S(2)}) %collective-permute-start.6) | collective-permute-done | bytes 131104 | tf_op jit(solution)/shard_map/ppermute | solution.py:114
  35.5 4.9 %collective-permute-done.7 = bf16[64,1024]{1,0:T(8,128)(2,1)S(1)} collective-permute-done((bf16[64,1024]{1,0:T(8,128)(2,1)S(1)}, bf16[64,1024]{1,0:T(8,128)(2,1)S(1)}, u32[]{:S(2)}, u32[]{:S(2)}) %collective-permute-start.7) | collective-permute-done | bytes 131104 | tf_op jit(solution)/shard_map/ppermute | solution.py:114
  50.3 3.5 %collective-permute-start.20 = (bf16[64,1024]{1,0:T(8,128)(2,1)S(1)}, bf16[64,1024]{1,0:T(8,128)(2,1)S(1)}, u32[]{:S(2)}, u32[]{:S(2)}) collective-permute-start(bf16[64,1024]{1,0:T(8,128)(2,1)S(1)} %fusion.55), channel_id=1, source_target_pairs={{0,3},{1,2},{2,1},{3,0},{4,7},{5,6},{6,5},{7,4},{8,11},{9,10},{10,... | collective-permute-start | bytes 393224 | tf_op jit(solution)/shard_map/ppermute | solution.py:114
  60.0 3.4 %collective-permute-start.22 = (bf16[64,1024]{1,0:T(8,128)(2,1)S(1)}, bf16[64,1024]{1,0:T(8,128)(2,1)S(1)}, u32[]{:S(2)}, u32[]{:S(2)}) collective-permute-start(bf16[64,1024]{1,0:T(8,128)(2,1)S(1)} %get-tuple-element.31), channel_id=1, source_target_pairs={{0,3},{1,2},{2,1},{3,0},{4,7},{5,6},{6,5},{7,4},{8,11},{9,10},{10,... | collective-permute-start | bytes 393224 | tf_op jit(solution)/shard_map/ppermute | solution.py:114
  63.8 4.2 %collective-permute-done.22 = bf16[64,1024]{1,0:T(8,128)(2,1)S(1)} collective-permute-done((bf16[64,1024]{1,0:T(8,128)(2,1)S(1)}, bf16[64,1024]{1,0:T(8,128)(2,1)S(1)}, u32[]{:S(2)}, u32[]{:S(2)}) %collective-permute-start.22) | collective-permute-done | bytes 131104 | tf_op jit(solution)/shard_map/ppermute | solution.py:114
  68.7 4.2 %collective-permute-done.23 = bf16[64,1024]{1,0:T(8,128)(2,1)S(1)} collective-permute-done((bf16[64,1024]{1,0:T(8,128)(2,1)S(1)}, bf16[64,1024]{1,0:T(8,128)(2,1)S(1)}, u32[]{:S(2)}, u32[]{:S(2)}) %collective-permute-start.23) | collective-permute-done | bytes 131104 | tf_op jit(solution)/shard_map/ppermute | solution.py:114
  82.9 2.8 %collective-permute-start.27 = (bf16[64,1024]{1,0:T(8,128)(2,1)S(1)}, bf16[64,1024]{1,0:T(8,128)(2,1)S(1)}, u32[]{:S(2)}, u32[]{:S(2)}) collective-permute-start(bf16[64,1024]{1,0:T(8,128)(2,1)S(1)} %fusion.54), channel_id=1, source_target_pairs={{0,3},{1,2},{2,1},{3,0},{4,7},{5,6},{6,5},{7,4},{8,11},{9,10},{10,... | collective-permute-start | bytes 393224 | tf_op jit(solution)/shard_map/ppermute | solution.py:114
  95.7 4.4 %collective-permute-done.29 = bf16[64,1024]{1,0:T(8,128)(2,1)S(1)} collective-permute-done((bf16[64,1024]{1,0:T(8,128)(2,1)S(1)}, bf16[64,1024]{1,0:T(8,128)(2,1)S(1)}, u32[]{:S(2)}, u32[]{:S(2)}) %collective-permute-start.29) | collective-permute-done | bytes 131104 | tf_op jit(solution)/shard_map/ppermute | solution.py:114
  100.1 4.9 %collective-permute-done.30 = bf16[64,1024]{1,0:T(8,128)(2,1)S(1)} collective-permute-done((bf16[64,1024]{1,0:T(8,128)(2,1)S(1)}, bf16[64,1024]{1,0:T(8,128)(2,1)S(1)}, u32[]{:S(2)}, u32[]{:S(2)}) %collective-permute-start.30) | collective-permute-done | bytes 131104 | tf_op jit(solution)/shard_map/ppermute | solution.py:114
  111.9 2.8 %collective-permute-start.34 = (bf16[32,2048]{1,0:T(8,128)(2,1)S(1)}, bf16[32,2048]{1,0:T(8,128)(2,1)S(1)}, u32[]{:S(2)}, u32[]{:S(2)}) collective-permute-start(bf16[32,2048]{1,0:T(8,128)(2,1)S(1)} %get-tuple-element.43), channel_id=1, source_target_pairs={{0,24},{4,28},{8,0},{12,4},{16,8},{20,12},{24,16},{28,20},{1,25},{... | collective-permute-start | bytes 393224 | tf_op jit(solution)/shard_map/ppermute | solution.py:91
  128.9 3.1 %collective-permute-done.50 = bf16[64,1024]{1,0:T(8,128)(2,1)S(1)} collective-permute-done((bf16[64,1024]{1,0:T(8,128)(2,1)S(1)}, bf16[64,1024]{1,0:T(8,128)(2,1)S(1)}, u32[]{:S(2)}, u32[]{:S(2)}) %collective-permute-start.50) | collective-permute-done | bytes 131104 | tf_op jit(solution)/shard_map/ppermute | solution.py:114
  132.8 4.3 %collective-permute-done.51 = bf16[64,1024]{1,0:T(8,128)(2,1)S(1)} collective-permute-done((bf16[64,1024]{1,0:T(8,128)(2,1)S(1)}, bf16[64,1024]{1,0:T(8,128)(2,1)S(1)}, u32[]{:S(2)}, u32[]{:S(2)}) %collective-permute-start.51) | collective-permute-done | bytes 131104 | tf_op jit(solution)/shard_map/ppermute | solution.py:114
  142.8 2.8 %collective-permute-start.63 = (bf16[32,2048]{1,0:T(8,128)(2,1)S(1)}, bf16[32,2048]{1,0:T(8,128)(2,1)S(1)}, u32[]{:S(2)}, u32[]{:S(2)}) collective-permute-start(bf16[32,2048]{1,0:T(8,128)(2,1)S(1)} %get-tuple-element.48), channel_id=1, source_target_pairs={{0,24},{4,28},{8,0},{12,4},{16,8},{20,12},{24,16},{28,20},{1,25},{... | collective-permute-start | bytes 393224 | tf_op jit(solution)/shard_map/ppermute | solution.py:91
  160.0 3.9 %collective-permute-done.57 = bf16[64,1024]{1,0:T(8,128)(2,1)S(1)} collective-permute-done((bf16[64,1024]{1,0:T(8,128)(2,1)S(1)}, bf16[64,1024]{1,0:T(8,128)(2,1)S(1)}, u32[]{:S(2)}, u32[]{:S(2)}) %collective-permute-start.57) | collective-permute-done | bytes 131104 | tf_op jit(solution)/shard_map/ppermute | solution.py:114
  168.1 4.1 %collective-permute-done.69 = bf16[64,1024]{1,0:T(8,128)(2,1)S(1)} collective-permute-done((bf16[64,1024]{1,0:T(8,128)(2,1)S(1)}, bf16[64,1024]{1,0:T(8,128)(2,1)S(1)}, u32[]{:S(2)}, u32[]{:S(2)}) %collective-permute-start.69) | collective-permute-done | bytes 131104 | tf_op jit(solution)/shard_map/ppermute | solution.py:114
  174.0 5.2 %collective-permute-done.70 = bf16[64,1024]{1,0:T(8,128)(2,1)S(1)} collective-permute-done((bf16[64,1024]{1,0:T(8,128)(2,1)S(1)}, bf16[64,1024]{1,0:T(8,128)(2,1)S(1)}, u32[]{:S(2)}, u32[]{:S(2)}) %collective-permute-start.70) | collective-permute-done | bytes 131104 | tf_op jit(solution)/shard_map/ppermute | solution.py:114
  182.6 5.4 %collective-permute-done.72 = bf16[64,1024]{1,0:T(8,128)(2,1)S(1)} collective-permute-done((bf16[64,1024]{1,0:T(8,128)(2,1)S(1)}, bf16[64,1024]{1,0:T(8,128)(2,1)S(1)}, u32[]{:S(2)}, u32[]{:S(2)}) %collective-permute-start.72) | collective-permute-done | bytes 131104 | tf_op jit(solution)/shard_map/ppermute | solution.py:114
  188.1 4.9 %collective-permute-done.73 = bf16[64,1024]{1,0:T(8,128)(2,1)S(1)} collective-permute-done((bf16[64,1024]{1,0:T(8,128)(2,1)S(1)}, bf16[64,1024]{1,0:T(8,128)(2,1)S(1)}, u32[]{:S(2)}, u32[]{:S(2)}) %collective-permute-start.73) | collective-permute-done | bytes 131104 | tf_op jit(solution)/shard_map/ppermute | solution.py:114
  197.1 3.3 %collective-permute-done.60 = bf16[64,1024]{1,0:T(8,128)(2,1)S(1)} collective-permute-done((bf16[64,1024]{1,0:T(8,128)(2,1)S(1)}, bf16[64,1024]{1,0:T(8,128)(2,1)S(1)}, u32[]{:S(2)}, u32[]{:S(2)}) %collective-permute-start.60) | collective-permute-done | bytes 131104 | tf_op jit(solution)/shard_map/ppermute | solution.py:81
  (276 shorter events, 107.1 us)
Async XLA Ops:
  9.4 13.7 %collective-permute-start.16 = (bf16[64,1024]{1,0:T(8,128)(2,1)S(1)}, bf16[64,1024]{1,0:T(8,128)(2,1)S(1)}, u32[]{:S(2)}, u32[]{:S(2)}) collective-permute-start(bf16[64,1024]{1,0:T(8,128)(2,1)S(1)} %bitcast.438), channel_id=1, source_target_pairs={{0,8},{4,12},{8,0},{12,4},{1,9},{5,13},{9,1},{13,5},{2,10},{6,14},... | collective-permute-start | bytes 393224 | tf_op jit(solution)/shard_map/ppermute | solution.py:81
  14.5 8.7 %collective-permute-start.2 = (bf16[64,1024]{1,0:T(8,128)(2,1)}, bf16[64,1024]{1,0:T(8,128)(2,1)S(1)}, u32[]{:S(2)}, u32[]{:S(2)}) collective-permute-start(bf16[64,1024]{1,0:T(8,128)(2,1)} %get-tuple-element.56), channel_id=1, source_target_pairs={{0,1},{1,0},{2,3},{3,2},{4,5},{5,4},{6,7},{7,6},{8,9},{9,8},{10,11... | collective-permute-start | bytes 393224 | tf_op jit(solution)/shard_map/ppermute | solution.py:114
  23.1 18.8 %collective-permute-start.17 = (bf16[2,64,1024]{2,1,0:T(8,128)(2,1)S(1)}, bf16[2,64,1024]{2,1,0:T(8,128)(2,1)S(1)}, u32[]{:S(2)}, u32[]{:S(2)}) collective-permute-start(bf16[2,64,1024]{2,1,0:T(8,128)(2,1)S(1)} %bitcast_dynamic-update-slice_fusion.44), channel_id=1, source_target_pairs={{0,4},{4,0},{8,12},{12,8},{1,5},{5,1},{9,13},{13,9},{2,6},{6,2},{1... | collective-permute-start | bytes 786440 | tf_op jit(solution)/shard_map/ppermute | solution.py:88
  26.5 9.0 %collective-permute-start.5 = (bf16[64,1024]{1,0:T(8,128)(2,1)S(1)}, bf16[64,1024]{1,0:T(8,128)(2,1)S(1)}, u32[]{:S(2)}, u32[]{:S(2)}) collective-permute-start(bf16[64,1024]{1,0:T(8,128)(2,1)S(1)} %get-tuple-element.33), channel_id=1, source_target_pairs={{0,1},{1,0},{2,3},{3,2},{4,5},{5,4},{6,7},{7,6},{8,9},{9,8},{10,11... | collective-permute-start | bytes 393224 | tf_op jit(solution)/shard_map/ppermute | solution.py:114
  44.0 15.5 %collective-permute-start.18 = (bf16[64,1024]{1,0:T(8,128)(2,1)S(1)}, bf16[64,1024]{1,0:T(8,128)(2,1)S(1)}, u32[]{:S(2)}, u32[]{:S(2)}) collective-permute-start(bf16[64,1024]{1,0:T(8,128)(2,1)S(1)} %get-tuple-element.40), channel_id=1, source_target_pairs={{0,1},{1,0},{2,3},{3,2},{4,5},{5,4},{6,7},{7,6},{8,9},{9,8},{10,11... | collective-permute-start | bytes 393224 | tf_op jit(solution)/shard_map/ppermute | solution.py:114
  50.3 9.2 %collective-permute-start.20 = (bf16[64,1024]{1,0:T(8,128)(2,1)S(1)}, bf16[64,1024]{1,0:T(8,128)(2,1)S(1)}, u32[]{:S(2)}, u32[]{:S(2)}) collective-permute-start(bf16[64,1024]{1,0:T(8,128)(2,1)S(1)} %fusion.55), channel_id=1, source_target_pairs={{0,3},{1,2},{2,1},{3,0},{4,7},{5,6},{6,5},{7,4},{8,11},{9,10},{10,... | collective-permute-start | bytes 393224 | tf_op jit(solution)/shard_map/ppermute | solution.py:114
  59.7 9.0 %collective-permute-start.21 = (bf16[64,1024]{1,0:T(8,128)(2,1)S(1)}, bf16[64,1024]{1,0:T(8,128)(2,1)S(1)}, u32[]{:S(2)}, u32[]{:S(2)}) collective-permute-start(bf16[64,1024]{1,0:T(8,128)(2,1)S(1)} %get-tuple-element.31), channel_id=1, source_target_pairs={{0,1},{1,0},{2,3},{3,2},{4,5},{5,4},{6,7},{7,6},{8,9},{9,8},{10,11... | collective-permute-start | bytes 393224 | tf_op jit(solution)/shard_map/ppermute | solution.py:114
  60.0 7.9 %collective-permute-start.22 = (bf16[64,1024]{1,0:T(8,128)(2,1)S(1)}, bf16[64,1024]{1,0:T(8,128)(2,1)S(1)}, u32[]{:S(2)}, u32[]{:S(2)}) collective-permute-start(bf16[64,1024]{1,0:T(8,128)(2,1)S(1)} %get-tuple-element.31), channel_id=1, source_target_pairs={{0,3},{1,2},{2,1},{3,0},{4,7},{5,6},{6,5},{7,4},{8,11},{9,10},{10,... | collective-permute-start | bytes 393224 | tf_op jit(solution)/shard_map/ppermute | solution.py:114
  63.5 10.9 %collective-permute-start.15 = (bf16[4,32,2048]{2,1,0:T(8,128)(2,1)S(1)}, bf16[4,32,2048]{2,1,0:T(8,128)(2,1)S(1)}, u32[]{:S(2)}, u32[]{:S(2)}) collective-permute-start(bf16[4,32,2048]{2,1,0:T(8,128)(2,1)S(1)} %bitcast_dynamic-update-slice_fusion.45), channel_id=1, source_target_pairs={{0,4},{4,0},{8,12},{12,8},{1,5},{5,1},{9,13},{13,9},{2,6},{6,2},{1... | collective-permute-start | bytes 1572872 | tf_op jit(solution)/shard_map/ppermute | solution.py:88
  77.4 8.2 %collective-permute-start.39 = (bf16[32,2048]{1,0:T(8,128)(2,1)S(1)}, bf16[32,2048]{1,0:T(8,128)(2,1)S(1)}, u32[]{:S(2)}, u32[]{:S(2)}) collective-permute-start(bf16[32,2048]{1,0:T(8,128)(2,1)S(1)} %get-tuple-element.53), channel_id=1, source_target_pairs={{0,8},{4,12},{8,16},{12,20},{16,24},{20,28},{24,0},{28,4},{1,9},{5... | collective-permute-start | bytes 393224 | tf_op jit(solution)/shard_map/ppermute | solution.py:91
  81.7 9.0 %collective-permute-start.25 = (bf16[64,1024]{1,0:T(8,128)(2,1)S(1)}, bf16[64,1024]{1,0:T(8,128)(2,1)S(1)}, u32[]{:S(2)}, u32[]{:S(2)}) collective-permute-start(bf16[64,1024]{1,0:T(8,128)(2,1)S(1)} %get-tuple-element.38), channel_id=1, source_target_pairs={{0,1},{1,0},{2,3},{3,2},{4,5},{5,4},{6,7},{7,6},{8,9},{9,8},{10,11... | collective-permute-start | bytes 393224 | tf_op jit(solution)/shard_map/ppermute | solution.py:114
  86.5 8.3 %collective-permute-start.42 = (bf16[32,2048]{1,0:T(8,128)(2,1)S(1)}, bf16[32,2048]{1,0:T(8,128)(2,1)S(1)}, u32[]{:S(2)}, u32[]{:S(2)}) collective-permute-start(bf16[32,2048]{1,0:T(8,128)(2,1)S(1)} %get-tuple-element.27), channel_id=1, source_target_pairs={{0,8},{4,12},{8,16},{12,20},{16,24},{20,28},{24,0},{28,4},{1,9},{5... | collective-permute-start | bytes 393224 | tf_op jit(solution)/shard_map/ppermute | solution.py:91
  90.8 9.3 %collective-permute-start.28 = (bf16[64,1024]{1,0:T(8,128)(2,1)S(1)}, bf16[64,1024]{1,0:T(8,128)(2,1)S(1)}, u32[]{:S(2)}, u32[]{:S(2)}) collective-permute-start(bf16[64,1024]{1,0:T(8,128)(2,1)S(1)} %get-tuple-element.21), channel_id=1, source_target_pairs={{0,1},{1,0},{2,3},{3,2},{4,5},{5,4},{6,7},{7,6},{8,9},{9,8},{10,11... | collective-permute-start | bytes 393224 | tf_op jit(solution)/shard_map/ppermute | solution.py:114
  92.1 8.0 %collective-permute-start.29 = (bf16[64,1024]{1,0:T(8,128)(2,1)S(1)}, bf16[64,1024]{1,0:T(8,128)(2,1)S(1)}, u32[]{:S(2)}, u32[]{:S(2)}) collective-permute-start(bf16[64,1024]{1,0:T(8,128)(2,1)S(1)} %get-tuple-element.21), channel_id=1, source_target_pairs={{0,3},{1,2},{2,1},{3,0},{4,7},{5,6},{6,5},{7,4},{8,11},{9,10},{10,... | collective-permute-start | bytes 393224 | tf_op jit(solution)/shard_map/ppermute | solution.py:114
  95.4 11.1 %collective-permute-start.45 = (bf16[4,32,2048]{2,1,0:T(8,128)(2,1)S(1)}, bf16[4,32,2048]{2,1,0:T(8,128)(2,1)S(1)}, u32[]{:S(2)}, u32[]{:S(2)}) collective-permute-start(bf16[4,32,2048]{2,1,0:T(8,128)(2,1)S(1)} %bitcast_dynamic-update-slice_fusion.28), channel_id=1, source_target_pairs={{0,4},{4,0},{8,12},{12,8},{1,5},{5,1},{9,13},{13,9},{2,6},{6,2},{1... | collective-permute-start | bytes 1572872 | tf_op jit(solution)/shard_map/ppermute | solution.py:88
  108.6 15.0 %collective-permute-start.46 = (bf16[64,1024]{1,0:T(8,128)(2,1)S(1)}, bf16[64,1024]{1,0:T(8,128)(2,1)S(1)}, u32[]{:S(2)}, u32[]{:S(2)}) collective-permute-start(bf16[64,1024]{1,0:T(8,128)(2,1)S(1)} %get-tuple-element.36), channel_id=1, source_target_pairs={{0,1},{1,0},{2,3},{3,2},{4,5},{5,4},{6,7},{7,6},{8,9},{9,8},{10,11... | collective-permute-start | bytes 393224 | tf_op jit(solution)/shard_map/ppermute | solution.py:114
  114.9 8.7 %collective-permute-start.48 = (bf16[64,1024]{1,0:T(8,128)(2,1)S(1)}, bf16[64,1024]{1,0:T(8,128)(2,1)S(1)}, u32[]{:S(2)}, u32[]{:S(2)}) collective-permute-start(bf16[64,1024]{1,0:T(8,128)(2,1)S(1)} %fusion.43), channel_id=1, source_target_pairs={{0,3},{1,2},{2,1},{3,0},{4,7},{5,6},{6,5},{7,4},{8,11},{9,10},{10,... | collective-permute-start | bytes 393224 | tf_op jit(solution)/shard_map/ppermute | solution.py:114
  123.7 9.0 %collective-permute-start.49 = (bf16[64,1024]{1,0:T(8,128)(2,1)S(1)}, bf16[64,1024]{1,0:T(8,128)(2,1)S(1)}, u32[]{:S(2)}, u32[]{:S(2)}) collective-permute-start(bf16[64,1024]{1,0:T(8,128)(2,1)S(1)} %get-tuple-element.19), channel_id=1, source_target_pairs={{0,1},{1,0},{2,3},{3,2},{4,5},{5,4},{6,7},{7,6},{8,9},{9,8},{10,11... | collective-permute-start | bytes 393224 | tf_op jit(solution)/shard_map/ppermute | solution.py:114
  128.7 9.9 %collective-permute-start.38 = (bf16[4,32,2048]{2,1,0:T(8,128)(2,1)S(1)}, bf16[4,32,2048]{2,1,0:T(8,128)(2,1)S(1)}, u32[]{:S(2)}, u32[]{:S(2)}) collective-permute-start(bf16[4,32,2048]{2,1,0:T(8,128)(2,1)S(1)} %bitcast_dynamic-update-slice_fusion.32), channel_id=1, source_target_pairs={{0,4},{4,0},{8,12},{12,8},{1,5},{5,1},{9,13},{13,9},{2,6},{6,2},{1... | collective-permute-start | bytes 1572872 | tf_op jit(solution)/shard_map/ppermute | solution.py:88
  145.6 9.0 %collective-permute-start.53 = (bf16[64,1024]{1,0:T(8,128)(2,1)S(1)}, bf16[64,1024]{1,0:T(8,128)(2,1)S(1)}, u32[]{:S(2)}, u32[]{:S(2)}) collective-permute-start(bf16[64,1024]{1,0:T(8,128)(2,1)S(1)} %get-tuple-element.34), channel_id=1, source_target_pairs={{0,1},{1,0},{2,3},{3,2},{4,5},{5,4},{6,7},{7,6},{8,9},{9,8},{10,11... | collective-permute-start | bytes 393224 | tf_op jit(solution)/shard_map/ppermute | solution.py:114
  154.8 9.7 %collective-permute-start.56 = (bf16[64,1024]{1,0:T(8,128)(2,1)S(1)}, bf16[64,1024]{1,0:T(8,128)(2,1)S(1)}, u32[]{:S(2)}, u32[]{:S(2)}) collective-permute-start(bf16[64,1024]{1,0:T(8,128)(2,1)S(1)} %get-tuple-element.5), channel_id=1, source_target_pairs={{0,1},{1,0},{2,3},{3,2},{4,5},{5,4},{6,7},{7,6},{8,9},{9,8},{10,11... | collective-permute-start | bytes 393224 | tf_op jit(solution)/shard_map/ppermute | solution.py:114
  163.8 10.0 %collective-permute-start.58 = (bf16[64,1024]{1,0:T(8,128)(2,1)S(1)}, bf16[64,1024]{1,0:T(8,128)(2,1)S(1)}, u32[]{:S(2)}, u32[]{:S(2)}) collective-permute-start(bf16[64,1024]{1,0:T(8,128)(2,1)S(1)} %collective-permute-done.57), channel_id=1, source_target_pairs={{0,1},{1,0},{2,3},{3,2},{4,5},{5,4},{6,7},{7,6},{8,9},{9,8},{10,11... | collective-permute-start | bytes 393224 | tf_op jit(solution)/shard_map/ppermute | solution.py:114
  179.3 8.7 %collective-permute-start.71 = (bf16[64,1024]{1,0:T(8,128)(2,1)S(1)}, bf16[64,1024]{1,0:T(8,128)(2,1)S(1)}, u32[]{:S(2)}, u32[]{:S(2)}) collective-permute-start(bf16[64,1024]{1,0:T(8,128)(2,1)S(1)} %get-tuple-element.12), channel_id=1, source_target_pairs={{0,1},{1,0},{2,3},{3,2},{4,5},{5,4},{6,7},{7,6},{8,9},{9,8},{10,11... | collective-permute-start | bytes 393224 | tf_op jit(solution)/shard_map/ppermute | solution.py:114
  182.5 11.4 %collective-permute-start.59 = (bf16[2,64,1024]{2,1,0:T(8,128)(2,1)S(1)}, bf16[2,64,1024]{2,1,0:T(8,128)(2,1)S(1)}, u32[]{:S(2)}, u32[]{:S(2)}) collective-permute-start(bf16[2,64,1024]{2,1,0:T(8,128)(2,1)S(1)} %fusion.29), channel_id=1, source_target_pairs={{0,4},{4,0},{8,12},{12,8},{1,5},{5,1},{9,13},{13,9},{2,6},{6,2},{1... | collective-permute-start | bytes 786440 | tf_op jit(solution)/shard_map/ppermute | solution.py:88
  (60 other events, 408.3 us)

commit v4 on v3

--- a/solution.py
+++ b/solution.py
@@ -75,13 +75,13 @@
     groups = layers * high
 
     def send_col(block, step):
-        return lax.ppermute(block, "col", [(i, (i + step) % cols) for i in range(cols)])
+        return lax.ppermute(block, "col", [(i, i ^ step) for i in range(cols)])
 
     def send_high(block, step):
         return lax.ppermute(
             block,
             "row",
-            [(i, (i // pair + step) % high * pair + i % pair) for i in range(rows)],
+            [(i, i ^ (step * pair)) for i in range(rows)],
         )
 
     def send_pair(block):
@@ -91,23 +91,20 @@
         return lax.ppermute(
             block,
             ("layer", "row"),
-            [
-                (i, (i // pair + step) % groups * pair + i % pair)
-                for i in range(layers * rows)
-            ],
+            [(i, i ^ (step * pair)) for i in range(layers * rows)],
         )
 
     def scatter(part, me, size, send):
         total = pick(part, me)
         low = part.astype(BF16)
-        got = [send(pick(low, (me + k) % size), k) for k in range(1, size)]
+        got = [send(pick(low, me ^ d), d) for d in range(size - 1, 0, -1)]
         for block in got:
             total = total + block.astype(F32)
         return total
 
     def gather(block, me, size, send):
         parts = [(me, block)]
-        parts += [((me - k) % size, send(block, k)) for k in range(1, size)]
+        parts += [(me ^ d, send(block, d)) for d in range(size - 1, 0, -1)]
         return place(parts), parts[-1][1]
 
     def swap_col(block, bits):

time: 204 us -> 201 us (0.985)
  waiting for transfers between devices: 89.3 us -> 82.8 us
  starting transfers between devices: 88.8 us -> 91.5 us
    ppermute x36, waiting for transfers between devices: 66.3 us -> 61.6 us  [swap_col(): return lax.ppermute(block, 'col', [(i, i ^ bits) for i in range(cols)])]
    ppermute x36, starting transfers between devices: 50.4 us -> 53.8 us  [swap_col(): return lax.ppermute(block, 'col', [(i, i ^ bits) for i in range(cols)])]
  transfers between devices with their start and end apart: 76 -> 76, of which waited for: 34 -> 33; matrix products, arithmetic and copies ran while one was open for 9% -> 10% of each run, Pallas kernels for 0% -> 0%
where the time goes in v4:
time: 201 us; the launch traced here: 200 us
  starting transfers between devices  91.5 us (46%)
  waiting for transfers between devices  82.8 us (41%)
  matrix products  13.6 us (7%)
  local copies, waits for them, and re-layouts  7.02 us (3%)
  other arithmetic  2.87 us (1%)
  between operations  2.64 us (1%)
    ppermute x36, waiting for transfers between devices, swap_col(): return lax.ppermute(block, 'col', [(i, i ^ bits) for i in range(cols)])  61.6 us
    ppermute x36, starting transfers between devices, swap_col(): return lax.ppermute(block, 'col', [(i, i ^ bits) for i in range(cols)])  53.8 us
    ppermute x24, starting transfers between devices, send_group(): lax.ppermute(block, ('layer', 'row'), [(i, i ^ step * pair) for i in rang...  28.4 us
    ppermute x24, waiting for transfers between devices, send_group(): lax.ppermute(block, ('layer', 'row'), [(i, i ^ step * pair) for i in rang...  11.7 us
    dot_general x10, matrix products, dot_nt(): lax.dot_general(a, b, (((1,), (1,)), ((), ())), preferred_element_type=F32)  11 us
    ppermute x4, starting transfers between devices, send_high(): lax.ppermute(block, 'row', [(i, i ^ step * pair) for i in range(rows)])  8.4 us
    ppermute x4, waiting for transfers between devices, send_high(): lax.ppermute(block, 'row', [(i, i ^ step * pair) for i in range(rows)])  8.06 us
  transfers between devices with their start and end apart: 76, of which 33 were waited for; matrix products, arithmetic and copies ran while one was open for 10% of the time, Pallas kernels for 0%

profile of v4, /device:TPU:0, one launch (start us, length us, event | category | flops | bytes accessed | tf_op | source)
XLA Modules:
  0.0 200.4 jit_solution(6623264068620061611)
XLA Ops:
  2.8 3.0 %collective-permute-start = (bf16[64,1024]{1,0:T(8,128)(2,1)S(1)}, bf16[64,1024]{1,0:T(8,128)(2,1)S(1)}, u32[]{:S(2)}, u32[]{:S(2)}) collective-permute-start(bf16[64,1024]{1,0:T(8,128)(2,1)S(1)} %bitcast.440), channel_id=1, source_target_pairs={{0,8},{4,12},{8,0},{12,4},{1,9},{5,13},{9,1},{13,5},{2,10},{6,14},... | collective-permute-start | bytes 393224 | tf_op jit(solution)/shard_map/ppermute | solution.py:81
  5.9 3.4 %collective-permute-done = bf16[64,1024]{1,0:T(8,128)(2,1)S(1)} collective-permute-done((bf16[64,1024]{1,0:T(8,128)(2,1)S(1)}, bf16[64,1024]{1,0:T(8,128)(2,1)S(1)}, u32[]{:S(2)}, u32[]{:S(2)}) %collective-permute-start) | collective-permute-done | bytes 131104 | tf_op jit(solution)/shard_map/ppermute | solution.py:81
  15.0 4.4 %collective-permute-done.3 = bf16[64,1024]{1,0:T(8,128)(2,1)S(1)} collective-permute-done((bf16[64,1024]{1,0:T(8,128)(2,1)}, bf16[64,1024]{1,0:T(8,128)(2,1)S(1)}, u32[]{:S(2)}, u32[]{:S(2)}) %collective-permute-start.3) | collective-permute-done | bytes 131104 | tf_op jit(solution)/shard_map/ppermute | solution.py:111
  19.4 3.7 %collective-permute-start.4 = (bf16[64,1024]{1,0:T(8,128)(2,1)S(1)}, bf16[64,1024]{1,0:T(8,128)(2,1)S(1)}, u32[]{:S(2)}, u32[]{:S(2)}) collective-permute-start(bf16[64,1024]{1,0:T(8,128)(2,1)S(1)} %fusion.62), channel_id=1, source_target_pairs={{0,3},{1,2},{2,1},{3,0},{4,7},{5,6},{6,5},{7,4},{8,11},{9,10},{10,... | collective-permute-start | bytes 393224 | tf_op jit(solution)/shard_map/ppermute | solution.py:111
  23.2 3.2 %collective-permute-done.4 = bf16[64,1024]{1,0:T(8,128)(2,1)S(1)} collective-permute-done((bf16[64,1024]{1,0:T(8,128)(2,1)S(1)}, bf16[64,1024]{1,0:T(8,128)(2,1)S(1)}, u32[]{:S(2)}, u32[]{:S(2)}) %collective-permute-start.4) | collective-permute-done | bytes 131104 | tf_op jit(solution)/shard_map/ppermute | solution.py:111
  28.3 2.7 %collective-permute-start.6 = (bf16[64,1024]{1,0:T(8,128)(2,1)S(1)}, bf16[64,1024]{1,0:T(8,128)(2,1)S(1)}, u32[]{:S(2)}, u32[]{:S(2)}) collective-permute-start(bf16[64,1024]{1,0:T(8,128)(2,1)S(1)} %get-tuple-element.33), channel_id=1, source_target_pairs={{0,3},{1,2},{2,1},{3,0},{4,7},{5,6},{6,5},{7,4},{8,11},{9,10},{10,... | collective-permute-start | bytes 393224 | tf_op jit(solution)/shard_map/ppermute | solution.py:111
  31.1 4.4 %collective-permute-done.6 = bf16[64,1024]{1,0:T(8,128)(2,1)S(1)} collective-permute-done((bf16[64,1024]{1,0:T(8,128)(2,1)S(1)}, bf16[64,1024]{1,0:T(8,128)(2,1)S(1)}, u32[]{:S(2)}, u32[]{:S(2)}) %collective-permute-start.6) | collective-permute-done | bytes 131104 | tf_op jit(solution)/shard_map/ppermute | solution.py:111
  35.5 4.9 %collective-permute-done.7 = bf16[64,1024]{1,0:T(8,128)(2,1)S(1)} collective-permute-done((bf16[64,1024]{1,0:T(8,128)(2,1)S(1)}, bf16[64,1024]{1,0:T(8,128)(2,1)S(1)}, u32[]{:S(2)}, u32[]{:S(2)}) %collective-permute-start.7) | collective-permute-done | bytes 131104 | tf_op jit(solution)/shard_map/ppermute | solution.py:111
  50.3 3.5 %collective-permute-start.20 = (bf16[64,1024]{1,0:T(8,128)(2,1)S(1)}, bf16[64,1024]{1,0:T(8,128)(2,1)S(1)}, u32[]{:S(2)}, u32[]{:S(2)}) collective-permute-start(bf16[64,1024]{1,0:T(8,128)(2,1)S(1)} %fusion.55), channel_id=1, source_target_pairs={{0,3},{1,2},{2,1},{3,0},{4,7},{5,6},{6,5},{7,4},{8,11},{9,10},{10,... | collective-permute-start | bytes 393224 | tf_op jit(solution)/shard_map/ppermute | solution.py:111
  59.6 3.5 %collective-permute-start.22 = (bf16[64,1024]{1,0:T(8,128)(2,1)S(1)}, bf16[64,1024]{1,0:T(8,128)(2,1)S(1)}, u32[]{:S(2)}, u32[]{:S(2)}) collective-permute-start(bf16[64,1024]{1,0:T(8,128)(2,1)S(1)} %get-tuple-element.31), channel_id=1, source_target_pairs={{0,3},{1,2},{2,1},{3,0},{4,7},{5,6},{6,5},{7,4},{8,11},{9,10},{10,... | collective-permute-start | bytes 393224 | tf_op jit(solution)/shard_map/ppermute | solution.py:111
  63.6 4.0 %collective-permute-done.22 = bf16[64,1024]{1,0:T(8,128)(2,1)S(1)} collective-permute-done((bf16[64,1024]{1,0:T(8,128)(2,1)S(1)}, bf16[64,1024]{1,0:T(8,128)(2,1)S(1)}, u32[]{:S(2)}, u32[]{:S(2)}) %collective-permute-start.22) | collective-permute-done | bytes 131104 | tf_op jit(solution)/shard_map/ppermute | solution.py:111
  68.5 4.1 %collective-permute-done.23 = bf16[64,1024]{1,0:T(8,128)(2,1)S(1)} collective-permute-done((bf16[64,1024]{1,0:T(8,128)(2,1)S(1)}, bf16[64,1024]{1,0:T(8,128)(2,1)S(1)}, u32[]{:S(2)}, u32[]{:S(2)}) %collective-permute-start.23) | collective-permute-done | bytes 131104 | tf_op jit(solution)/shard_map/ppermute | solution.py:111
  82.0 2.8 %collective-permute-start.27 = (bf16[64,1024]{1,0:T(8,128)(2,1)S(1)}, bf16[64,1024]{1,0:T(8,128)(2,1)S(1)}, u32[]{:S(2)}, u32[]{:S(2)}) collective-permute-start(bf16[64,1024]{1,0:T(8,128)(2,1)S(1)} %fusion.54), channel_id=1, source_target_pairs={{0,3},{1,2},{2,1},{3,0},{4,7},{5,6},{6,5},{7,4},{8,11},{9,10},{10,... | collective-permute-start | bytes 393224 | tf_op jit(solution)/shard_map/ppermute | solution.py:111
  91.2 2.7 %collective-permute-start.29 = (bf16[64,1024]{1,0:T(8,128)(2,1)S(1)}, bf16[64,1024]{1,0:T(8,128)(2,1)S(1)}, u32[]{:S(2)}, u32[]{:S(2)}) collective-permute-start(bf16[64,1024]{1,0:T(8,128)(2,1)S(1)} %get-tuple-element.21), channel_id=1, source_target_pairs={{0,3},{1,2},{2,1},{3,0},{4,7},{5,6},{6,5},{7,4},{8,11},{9,10},{10,... | collective-permute-start | bytes 393224 | tf_op jit(solution)/shard_map/ppermute | solution.py:111
  95.1 3.5 %collective-permute-done.29 = bf16[64,1024]{1,0:T(8,128)(2,1)S(1)} collective-permute-done((bf16[64,1024]{1,0:T(8,128)(2,1)S(1)}, bf16[64,1024]{1,0:T(8,128)(2,1)S(1)}, u32[]{:S(2)}, u32[]{:S(2)}) %collective-permute-start.29) | collective-permute-done | bytes 131104 | tf_op jit(solution)/shard_map/ppermute | solution.py:111
  98.6 4.9 %collective-permute-done.30 = bf16[64,1024]{1,0:T(8,128)(2,1)S(1)} collective-permute-done((bf16[64,1024]{1,0:T(8,128)(2,1)S(1)}, bf16[64,1024]{1,0:T(8,128)(2,1)S(1)}, u32[]{:S(2)}, u32[]{:S(2)}) %collective-permute-start.30) | collective-permute-done | bytes 131104 | tf_op jit(solution)/shard_map/ppermute | solution.py:111
  122.5 2.9 %collective-permute-start.50 = (bf16[64,1024]{1,0:T(8,128)(2,1)S(1)}, bf16[64,1024]{1,0:T(8,128)(2,1)S(1)}, u32[]{:S(2)}, u32[]{:S(2)}) collective-permute-start(bf16[64,1024]{1,0:T(8,128)(2,1)S(1)} %get-tuple-element.19), channel_id=1, source_target_pairs={{0,3},{1,2},{2,1},{3,0},{4,7},{5,6},{6,5},{7,4},{8,11},{9,10},{10,... | collective-permute-start | bytes 393224 | tf_op jit(solution)/shard_map/ppermute | solution.py:111
  130.1 4.9 %collective-permute-done.51 = bf16[64,1024]{1,0:T(8,128)(2,1)S(1)} collective-permute-done((bf16[64,1024]{1,0:T(8,128)(2,1)S(1)}, bf16[64,1024]{1,0:T(8,128)(2,1)S(1)}, u32[]{:S(2)}, u32[]{:S(2)}) %collective-permute-start.51) | collective-permute-done | bytes 131104 | tf_op jit(solution)/shard_map/ppermute | solution.py:111
  157.9 3.0 %collective-permute-done.57 = bf16[64,1024]{1,0:T(8,128)(2,1)S(1)} collective-permute-done((bf16[64,1024]{1,0:T(8,128)(2,1)S(1)}, bf16[64,1024]{1,0:T(8,128)(2,1)S(1)}, u32[]{:S(2)}, u32[]{:S(2)}) %collective-permute-start.57) | collective-permute-done | bytes 131104 | tf_op jit(solution)/shard_map/ppermute | solution.py:111
  164.6 4.9 %collective-permute-done.69 = bf16[64,1024]{1,0:T(8,128)(2,1)S(1)} collective-permute-done((bf16[64,1024]{1,0:T(8,128)(2,1)S(1)}, bf16[64,1024]{1,0:T(8,128)(2,1)S(1)}, u32[]{:S(2)}, u32[]{:S(2)}) %collective-permute-start.69) | collective-permute-done | bytes 131104 | tf_op jit(solution)/shard_map/ppermute | solution.py:111
  172.0 4.6 %collective-permute-done.70 = bf16[64,1024]{1,0:T(8,128)(2,1)S(1)} collective-permute-done((bf16[64,1024]{1,0:T(8,128)(2,1)S(1)}, bf16[64,1024]{1,0:T(8,128)(2,1)S(1)}, u32[]{:S(2)}, u32[]{:S(2)}) %collective-permute-start.70) | collective-permute-done | bytes 131104 | tf_op jit(solution)/shard_map/ppermute | solution.py:111
  176.9 2.8 %collective-permute-start.72 = (bf16[64,1024]{1,0:T(8,128)(2,1)S(1)}, bf16[64,1024]{1,0:T(8,128)(2,1)S(1)}, u32[]{:S(2)}, u32[]{:S(2)}) collective-permute-start(bf16[64,1024]{1,0:T(8,128)(2,1)S(1)} %get-tuple-element.12), channel_id=1, source_target_pairs={{0,3},{1,2},{2,1},{3,0},{4,7},{5,6},{6,5},{7,4},{8,11},{9,10},{10,... | collective-permute-start | bytes 393224 | tf_op jit(solution)/shard_map/ppermute | solution.py:111
  180.6 3.5 %collective-permute-done.72 = bf16[64,1024]{1,0:T(8,128)(2,1)S(1)} collective-permute-done((bf16[64,1024]{1,0:T(8,128)(2,1)S(1)}, bf16[64,1024]{1,0:T(8,128)(2,1)S(1)}, u32[]{:S(2)}, u32[]{:S(2)}) %collective-permute-start.72) | collective-permute-done | bytes 131104 | tf_op jit(solution)/shard_map/ppermute | solution.py:111
  185.3 3.7 %collective-permute-done.73 = bf16[64,1024]{1,0:T(8,128)(2,1)S(1)} collective-permute-done((bf16[64,1024]{1,0:T(8,128)(2,1)S(1)}, bf16[64,1024]{1,0:T(8,128)(2,1)S(1)}, u32[]{:S(2)}, u32[]{:S(2)}) %collective-permute-start.73) | collective-permute-done | bytes 131104 | tf_op jit(solution)/shard_map/ppermute | solution.py:111
  (276 shorter events, 108.8 us)
Async XLA Ops:
  9.4 13.7 %collective-permute-start.16 = (bf16[64,1024]{1,0:T(8,128)(2,1)S(1)}, bf16[64,1024]{1,0:T(8,128)(2,1)S(1)}, u32[]{:S(2)}, u32[]{:S(2)}) collective-permute-start(bf16[64,1024]{1,0:T(8,128)(2,1)S(1)} %bitcast.438), channel_id=1, source_target_pairs={{0,8},{4,12},{8,0},{12,4},{1,9},{5,13},{9,1},{13,5},{2,10},{6,14},... | collective-permute-start | bytes 393224 | tf_op jit(solution)/shard_map/ppermute | solution.py:81
  14.5 8.7 %collective-permute-start.2 = (bf16[64,1024]{1,0:T(8,128)(2,1)}, bf16[64,1024]{1,0:T(8,128)(2,1)S(1)}, u32[]{:S(2)}, u32[]{:S(2)}) collective-permute-start(bf16[64,1024]{1,0:T(8,128)(2,1)} %get-tuple-element.56), channel_id=1, source_target_pairs={{0,1},{1,0},{2,3},{3,2},{4,5},{5,4},{6,7},{7,6},{8,9},{9,8},{10,11... | collective-permute-start | bytes 393224 | tf_op jit(solution)/shard_map/ppermute | solution.py:111
  23.1 18.8 %collective-permute-start.17 = (bf16[2,64,1024]{2,1,0:T(8,128)(2,1)S(1)}, bf16[2,64,1024]{2,1,0:T(8,128)(2,1)S(1)}, u32[]{:S(2)}, u32[]{:S(2)}) collective-permute-start(bf16[2,64,1024]{2,1,0:T(8,128)(2,1)S(1)} %bitcast_dynamic-update-slice_fusion.44), channel_id=1, source_target_pairs={{0,4},{4,0},{8,12},{12,8},{1,5},{5,1},{9,13},{13,9},{2,6},{6,2},{1... | collective-permute-start | bytes 786440 | tf_op jit(solution)/shard_map/ppermute | solution.py:88
  26.5 9.0 %collective-permute-start.5 = (bf16[64,1024]{1,0:T(8,128)(2,1)S(1)}, bf16[64,1024]{1,0:T(8,128)(2,1)S(1)}, u32[]{:S(2)}, u32[]{:S(2)}) collective-permute-start(bf16[64,1024]{1,0:T(8,128)(2,1)S(1)} %get-tuple-element.33), channel_id=1, source_target_pairs={{0,1},{1,0},{2,3},{3,2},{4,5},{5,4},{6,7},{7,6},{8,9},{9,8},{10,11... | collective-permute-start | bytes 393224 | tf_op jit(solution)/shard_map/ppermute | solution.py:111
  44.0 15.3 %collective-permute-start.18 = (bf16[64,1024]{1,0:T(8,128)(2,1)S(1)}, bf16[64,1024]{1,0:T(8,128)(2,1)S(1)}, u32[]{:S(2)}, u32[]{:S(2)}) collective-permute-start(bf16[64,1024]{1,0:T(8,128)(2,1)S(1)} %get-tuple-element.40), channel_id=1, source_target_pairs={{0,1},{1,0},{2,3},{3,2},{4,5},{5,4},{6,7},{7,6},{8,9},{9,8},{10,11... | collective-permute-start | bytes 393224 | tf_op jit(solution)/shard_map/ppermute | solution.py:111
  50.3 9.0 %collective-permute-start.20 = (bf16[64,1024]{1,0:T(8,128)(2,1)S(1)}, bf16[64,1024]{1,0:T(8,128)(2,1)S(1)}, u32[]{:S(2)}, u32[]{:S(2)}) collective-permute-start(bf16[64,1024]{1,0:T(8,128)(2,1)S(1)} %fusion.55), channel_id=1, source_target_pairs={{0,3},{1,2},{2,1},{3,0},{4,7},{5,6},{6,5},{7,4},{8,11},{9,10},{10,... | collective-permute-start | bytes 393224 | tf_op jit(solution)/shard_map/ppermute | solution.py:111
  59.4 9.0 %collective-permute-start.21 = (bf16[64,1024]{1,0:T(8,128)(2,1)S(1)}, bf16[64,1024]{1,0:T(8,128)(2,1)S(1)}, u32[]{:S(2)}, u32[]{:S(2)}) collective-permute-start(bf16[64,1024]{1,0:T(8,128)(2,1)S(1)} %get-tuple-element.31), channel_id=1, source_target_pairs={{0,1},{1,0},{2,3},{3,2},{4,5},{5,4},{6,7},{7,6},{8,9},{9,8},{10,11... | collective-permute-start | bytes 393224 | tf_op jit(solution)/shard_map/ppermute | solution.py:111
  59.6 8.0 %collective-permute-start.22 = (bf16[64,1024]{1,0:T(8,128)(2,1)S(1)}, bf16[64,1024]{1,0:T(8,128)(2,1)S(1)}, u32[]{:S(2)}, u32[]{:S(2)}) collective-permute-start(bf16[64,1024]{1,0:T(8,128)(2,1)S(1)} %get-tuple-element.31), channel_id=1, source_target_pairs={{0,3},{1,2},{2,1},{3,0},{4,7},{5,6},{6,5},{7,4},{8,11},{9,10},{10,... | collective-permute-start | bytes 393224 | tf_op jit(solution)/shard_map/ppermute | solution.py:111
  63.3 10.7 %collective-permute-start.15 = (bf16[4,32,2048]{2,1,0:T(8,128)(2,1)S(1)}, bf16[4,32,2048]{2,1,0:T(8,128)(2,1)S(1)}, u32[]{:S(2)}, u32[]{:S(2)}) collective-permute-start(bf16[4,32,2048]{2,1,0:T(8,128)(2,1)S(1)} %bitcast_dynamic-update-slice_fusion.45), channel_id=1, source_target_pairs={{0,4},{4,0},{8,12},{12,8},{1,5},{5,1},{9,13},{13,9},{2,6},{6,2},{1... | collective-permute-start | bytes 1572872 | tf_op jit(solution)/shard_map/ppermute | solution.py:88
  80.8 9.0 %collective-permute-start.25 = (bf16[64,1024]{1,0:T(8,128)(2,1)S(1)}, bf16[64,1024]{1,0:T(8,128)(2,1)S(1)}, u32[]{:S(2)}, u32[]{:S(2)}) collective-permute-start(bf16[64,1024]{1,0:T(8,128)(2,1)S(1)} %get-tuple-element.38), channel_id=1, source_target_pairs={{0,1},{1,0},{2,3},{3,2},{4,5},{5,4},{6,7},{7,6},{8,9},{9,8},{10,11... | collective-permute-start | bytes 393224 | tf_op jit(solution)/shard_map/ppermute | solution.py:111
  82.0 7.8 %collective-permute-start.27 = (bf16[64,1024]{1,0:T(8,128)(2,1)S(1)}, bf16[64,1024]{1,0:T(8,128)(2,1)S(1)}, u32[]{:S(2)}, u32[]{:S(2)}) collective-permute-start(bf16[64,1024]{1,0:T(8,128)(2,1)S(1)} %fusion.54), channel_id=1, source_target_pairs={{0,3},{1,2},{2,1},{3,0},{4,7},{5,6},{6,5},{7,4},{8,11},{9,10},{10,... | collective-permute-start | bytes 393224 | tf_op jit(solution)/shard_map/ppermute | solution.py:111
  90.0 8.6 %collective-permute-start.28 = (bf16[64,1024]{1,0:T(8,128)(2,1)S(1)}, bf16[64,1024]{1,0:T(8,128)(2,1)S(1)}, u32[]{:S(2)}, u32[]{:S(2)}) collective-permute-start(bf16[64,1024]{1,0:T(8,128)(2,1)S(1)} %get-tuple-element.21), channel_id=1, source_target_pairs={{0,1},{1,0},{2,3},{3,2},{4,5},{5,4},{6,7},{7,6},{8,9},{9,8},{10,11... | collective-permute-start | bytes 393224 | tf_op jit(solution)/shard_map/ppermute | solution.py:111
  94.8 10.2 %collective-permute-start.45 = (bf16[4,32,2048]{2,1,0:T(8,128)(2,1)S(1)}, bf16[4,32,2048]{2,1,0:T(8,128)(2,1)S(1)}, u32[]{:S(2)}, u32[]{:S(2)}) collective-permute-start(bf16[4,32,2048]{2,1,0:T(8,128)(2,1)S(1)} %bitcast_dynamic-update-slice_fusion.28), channel_id=1, source_target_pairs={{0,4},{4,0},{8,12},{12,8},{1,5},{5,1},{9,13},{13,9},{2,6},{6,2},{1... | collective-permute-start | bytes 1572872 | tf_op jit(solution)/shard_map/ppermute | solution.py:88
  107.1 14.8 %collective-permute-start.46 = (bf16[64,1024]{1,0:T(8,128)(2,1)S(1)}, bf16[64,1024]{1,0:T(8,128)(2,1)S(1)}, u32[]{:S(2)}, u32[]{:S(2)}) collective-permute-start(bf16[64,1024]{1,0:T(8,128)(2,1)S(1)} %get-tuple-element.36), channel_id=1, source_target_pairs={{0,1},{1,0},{2,3},{3,2},{4,5},{5,4},{6,7},{7,6},{8,9},{9,8},{10,11... | collective-permute-start | bytes 393224 | tf_op jit(solution)/shard_map/ppermute | solution.py:111
  113.4 8.5 %collective-permute-start.48 = (bf16[64,1024]{1,0:T(8,128)(2,1)S(1)}, bf16[64,1024]{1,0:T(8,128)(2,1)S(1)}, u32[]{:S(2)}, u32[]{:S(2)}) collective-permute-start(bf16[64,1024]{1,0:T(8,128)(2,1)S(1)} %fusion.43), channel_id=1, source_target_pairs={{0,3},{1,2},{2,1},{3,0},{4,7},{5,6},{6,5},{7,4},{8,11},{9,10},{10,... | collective-permute-start | bytes 393224 | tf_op jit(solution)/shard_map/ppermute | solution.py:111
  122.0 8.0 %collective-permute-start.49 = (bf16[64,1024]{1,0:T(8,128)(2,1)S(1)}, bf16[64,1024]{1,0:T(8,128)(2,1)S(1)}, u32[]{:S(2)}, u32[]{:S(2)}) collective-permute-start(bf16[64,1024]{1,0:T(8,128)(2,1)S(1)} %get-tuple-element.19), channel_id=1, source_target_pairs={{0,1},{1,0},{2,3},{3,2},{4,5},{5,4},{6,7},{7,6},{8,9},{9,8},{10,11... | collective-permute-start | bytes 393224 | tf_op jit(solution)/shard_map/ppermute | solution.py:111
  127.2 9.3 %collective-permute-start.38 = (bf16[4,32,2048]{2,1,0:T(8,128)(2,1)S(1)}, bf16[4,32,2048]{2,1,0:T(8,128)(2,1)S(1)}, u32[]{:S(2)}, u32[]{:S(2)}) collective-permute-start(bf16[4,32,2048]{2,1,0:T(8,128)(2,1)S(1)} %bitcast_dynamic-update-slice_fusion.32), channel_id=1, source_target_pairs={{0,4},{4,0},{8,12},{12,8},{1,5},{5,1},{9,13},{13,9},{2,6},{6,2},{1... | collective-permute-start | bytes 1572872 | tf_op jit(solution)/shard_map/ppermute | solution.py:88
  138.8 7.9 %collective-permute-start.61 = (bf16[32,2048]{1,0:T(8,128)(2,1)S(1)}, bf16[32,2048]{1,0:T(8,128)(2,1)S(1)}, u32[]{:S(2)}, u32[]{:S(2)}) collective-permute-start(bf16[32,2048]{1,0:T(8,128)(2,1)S(1)} %get-tuple-element.47), channel_id=1, source_target_pairs={{0,24},{4,28},{8,16},{12,20},{16,8},{20,12},{24,0},{28,4},{1,25},{... | collective-permute-start | bytes 393224 | tf_op jit(solution)/shard_map/ppermute | solution.py:91
  140.3 8.0 %collective-permute-start.62 = (bf16[32,2048]{1,0:T(8,128)(2,1)S(1)}, bf16[32,2048]{1,0:T(8,128)(2,1)S(1)}, u32[]{:S(2)}, u32[]{:S(2)}) collective-permute-start(bf16[32,2048]{1,0:T(8,128)(2,1)S(1)} %get-tuple-element.49), channel_id=1, source_target_pairs={{0,16},{4,20},{8,24},{12,28},{16,0},{20,4},{24,8},{28,12},{1,17},{... | collective-permute-start | bytes 393224 | tf_op jit(solution)/shard_map/ppermute | solution.py:91
  142.4 9.6 %collective-permute-start.53 = (bf16[64,1024]{1,0:T(8,128)(2,1)S(1)}, bf16[64,1024]{1,0:T(8,128)(2,1)S(1)}, u32[]{:S(2)}, u32[]{:S(2)}) collective-permute-start(bf16[64,1024]{1,0:T(8,128)(2,1)S(1)} %get-tuple-element.34), channel_id=1, source_target_pairs={{0,1},{1,0},{2,3},{3,2},{4,5},{5,4},{6,7},{7,6},{8,9},{9,8},{10,11... | collective-permute-start | bytes 393224 | tf_op jit(solution)/shard_map/ppermute | solution.py:111
  152.1 8.8 %collective-permute-start.56 = (bf16[64,1024]{1,0:T(8,128)(2,1)S(1)}, bf16[64,1024]{1,0:T(8,128)(2,1)S(1)}, u32[]{:S(2)}, u32[]{:S(2)}) collective-permute-start(bf16[64,1024]{1,0:T(8,128)(2,1)S(1)} %get-tuple-element.5), channel_id=1, source_target_pairs={{0,1},{1,0},{2,3},{3,2},{4,5},{5,4},{6,7},{7,6},{8,9},{9,8},{10,11... | collective-permute-start | bytes 393224 | tf_op jit(solution)/shard_map/ppermute | solution.py:111
  160.9 11.1 %collective-permute-start.58 = (bf16[64,1024]{1,0:T(8,128)(2,1)S(1)}, bf16[64,1024]{1,0:T(8,128)(2,1)S(1)}, u32[]{:S(2)}, u32[]{:S(2)}) collective-permute-start(bf16[64,1024]{1,0:T(8,128)(2,1)S(1)} %collective-permute-done.57), channel_id=1, source_target_pairs={{0,1},{1,0},{2,3},{3,2},{4,5},{5,4},{6,7},{7,6},{8,9},{9,8},{10,11... | collective-permute-start | bytes 393224 | tf_op jit(solution)/shard_map/ppermute | solution.py:111
  176.8 8.5 %collective-permute-start.71 = (bf16[64,1024]{1,0:T(8,128)(2,1)S(1)}, bf16[64,1024]{1,0:T(8,128)(2,1)S(1)}, u32[]{:S(2)}, u32[]{:S(2)}) collective-permute-start(bf16[64,1024]{1,0:T(8,128)(2,1)S(1)} %get-tuple-element.12), channel_id=1, source_target_pairs={{0,1},{1,0},{2,3},{3,2},{4,5},{5,4},{6,7},{7,6},{8,9},{9,8},{10,11... | collective-permute-start | bytes 393224 | tf_op jit(solution)/shard_map/ppermute | solution.py:111
  180.5 9.5 %collective-permute-start.59 = (bf16[2,64,1024]{2,1,0:T(8,128)(2,1)S(1)}, bf16[2,64,1024]{2,1,0:T(8,128)(2,1)S(1)}, u32[]{:S(2)}, u32[]{:S(2)}) collective-permute-start(bf16[2,64,1024]{2,1,0:T(8,128)(2,1)S(1)} %fusion.29), channel_id=1, source_target_pairs={{0,4},{4,0},{8,12},{12,8},{1,5},{5,1},{9,13},{13,9},{2,6},{6,2},{1... | collective-permute-start | bytes 786440 | tf_op jit(solution)/shard_map/ppermute | solution.py:88
  (60 other events, 400.5 us)

commit v5 on v4

--- a/solution.py
+++ b/solution.py
@@ -18,7 +18,7 @@
     return out
 
 
-WAITS = (1, None, None, None)
+WAITS = (1, None, 2, None)
 
 
 def alone(steps):

time: 201 us -> 201 us (level)
  transfers between devices with their start and end apart: 76 -> 76, of which waited for: 33 -> 35; matrix products, arithmetic and copies ran while one was open for 10% -> 10% of each run, Pallas kernels for 0% -> 0%
where the time goes in v5:
time: 201 us
  starting transfers between devices  90 us (45%)
  waiting for transfers between devices  84.8 us (42%)
  matrix products  13.5 us (7%)
  local copies, waits for them, and re-layouts  7 us (3%)
  other arithmetic  3.02 us (2%)
  between operations  2.68 us (1%)
    ppermute x36, waiting for transfers between devices, swap_col(): return lax.ppermute(block, 'col', [(i, i ^ bits) for i in range(cols)])  62.5 us
    ppermute x36, starting transfers between devices, swap_col(): return lax.ppermute(block, 'col', [(i, i ^ bits) for i in range(cols)])  53.4 us
    ppermute x24, starting transfers between devices, send_group(): lax.ppermute(block, ('layer', 'row'), [(i, i ^ step * pair) for i in rang...  28.4 us
    ppermute x24, waiting for transfers between devices, send_group(): lax.ppermute(block, ('layer', 'row'), [(i, i ^ step * pair) for i in rang...  12.1 us
    dot_general x10, matrix products, dot_nt(): lax.dot_general(a, b, (((1,), (1,)), ((), ())), preferred_element_type=F32)  11 us
    ppermute x4, waiting for transfers between devices, send_high(): lax.ppermute(block, 'row', [(i, i ^ step * pair) for i in range(rows)])  8.6 us
    ppermute x4, starting transfers between devices, send_high(): lax.ppermute(block, 'row', [(i, i ^ step * pair) for i in range(rows)])  7.38 us
  transfers between devices with their start and end apart: 76, of which 35 were waited for; matrix products, arithmetic and copies ran while one was open for 10% of the time, Pallas kernels for 0%

profile of v5, /device:TPU:0, one launch (start us, length us, event | category | flops | bytes accessed | tf_op | source)
XLA Modules:
  0.0 201.0 jit_solution(4634528993654033956)
XLA Ops:
  2.8 3.0 %collective-permute-start = (bf16[64,1024]{1,0:T(8,128)(2,1)S(1)}, bf16[64,1024]{1,0:T(8,128)(2,1)S(1)}, u32[]{:S(2)}, u32[]{:S(2)}) collective-permute-start(bf16[64,1024]{1,0:T(8,128)(2,1)S(1)} %bitcast.442), channel_id=1, source_target_pairs={{0,8},{4,12},{8,0},{12,4},{1,9},{5,13},{9,1},{13,5},{2,10},{6,14},... | collective-permute-start | bytes 393224 | tf_op jit(solution)/shard_map/ppermute | solution.py:81
  5.9 3.4 %collective-permute-done = bf16[64,1024]{1,0:T(8,128)(2,1)S(1)} collective-permute-done((bf16[64,1024]{1,0:T(8,128)(2,1)S(1)}, bf16[64,1024]{1,0:T(8,128)(2,1)S(1)}, u32[]{:S(2)}, u32[]{:S(2)}) %collective-permute-start) | collective-permute-done | bytes 131104 | tf_op jit(solution)/shard_map/ppermute | solution.py:81
  15.0 4.4 %collective-permute-done.3 = bf16[64,1024]{1,0:T(8,128)(2,1)S(1)} collective-permute-done((bf16[64,1024]{1,0:T(8,128)(2,1)}, bf16[64,1024]{1,0:T(8,128)(2,1)S(1)}, u32[]{:S(2)}, u32[]{:S(2)}) %collective-permute-start.3) | collective-permute-done | bytes 131104 | tf_op jit(solution)/shard_map/ppermute | solution.py:111
  19.4 3.7 %collective-permute-start.4 = (bf16[64,1024]{1,0:T(8,128)(2,1)S(1)}, bf16[64,1024]{1,0:T(8,128)(2,1)S(1)}, u32[]{:S(2)}, u32[]{:S(2)}) collective-permute-start(bf16[64,1024]{1,0:T(8,128)(2,1)S(1)} %fusion.62), channel_id=1, source_target_pairs={{0,3},{1,2},{2,1},{3,0},{4,7},{5,6},{6,5},{7,4},{8,11},{9,10},{10,... | collective-permute-start | bytes 393224 | tf_op jit(solution)/shard_map/ppermute | solution.py:111
  23.2 3.2 %collective-permute-done.4 = bf16[64,1024]{1,0:T(8,128)(2,1)S(1)} collective-permute-done((bf16[64,1024]{1,0:T(8,128)(2,1)S(1)}, bf16[64,1024]{1,0:T(8,128)(2,1)S(1)}, u32[]{:S(2)}, u32[]{:S(2)}) %collective-permute-start.4) | collective-permute-done | bytes 131104 | tf_op jit(solution)/shard_map/ppermute | solution.py:111
  28.4 2.7 %collective-permute-start.6 = (bf16[64,1024]{1,0:T(8,128)(2,1)S(1)}, bf16[64,1024]{1,0:T(8,128)(2,1)S(1)}, u32[]{:S(2)}, u32[]{:S(2)}) collective-permute-start(bf16[64,1024]{1,0:T(8,128)(2,1)S(1)} %get-tuple-element.35), channel_id=1, source_target_pairs={{0,3},{1,2},{2,1},{3,0},{4,7},{5,6},{6,5},{7,4},{8,11},{9,10},{10,... | collective-permute-start | bytes 393224 | tf_op jit(solution)/shard_map/ppermute | solution.py:111
  31.1 4.4 %collective-permute-done.6 = bf16[64,1024]{1,0:T(8,128)(2,1)S(1)} collective-permute-done((bf16[64,1024]{1,0:T(8,128)(2,1)S(1)}, bf16[64,1024]{1,0:T(8,128)(2,1)S(1)}, u32[]{:S(2)}, u32[]{:S(2)}) %collective-permute-start.6) | collective-permute-done | bytes 131104 | tf_op jit(solution)/shard_map/ppermute | solution.py:111
  35.5 4.9 %collective-permute-done.7 = bf16[64,1024]{1,0:T(8,128)(2,1)S(1)} collective-permute-done((bf16[64,1024]{1,0:T(8,128)(2,1)S(1)}, bf16[64,1024]{1,0:T(8,128)(2,1)S(1)}, u32[]{:S(2)}, u32[]{:S(2)}) %collective-permute-start.7) | collective-permute-done | bytes 131104 | tf_op jit(solution)/shard_map/ppermute | solution.py:111
  50.3 3.5 %collective-permute-start.20 = (bf16[64,1024]{1,0:T(8,128)(2,1)S(1)}, bf16[64,1024]{1,0:T(8,128)(2,1)S(1)}, u32[]{:S(2)}, u32[]{:S(2)}) collective-permute-start(bf16[64,1024]{1,0:T(8,128)(2,1)S(1)} %fusion.55), channel_id=1, source_target_pairs={{0,3},{1,2},{2,1},{3,0},{4,7},{5,6},{6,5},{7,4},{8,11},{9,10},{10,... | collective-permute-start | bytes 393224 | tf_op jit(solution)/shard_map/ppermute | solution.py:111
  59.6 3.5 %collective-permute-start.22 = (bf16[64,1024]{1,0:T(8,128)(2,1)S(1)}, bf16[64,1024]{1,0:T(8,128)(2,1)S(1)}, u32[]{:S(2)}, u32[]{:S(2)}) collective-permute-start(bf16[64,1024]{1,0:T(8,128)(2,1)S(1)} %get-tuple-element.31), channel_id=1, source_target_pairs={{0,3},{1,2},{2,1},{3,0},{4,7},{5,6},{6,5},{7,4},{8,11},{9,10},{10,... | collective-permute-start | bytes 393224 | tf_op jit(solution)/shard_map/ppermute | solution.py:111
  63.6 4.0 %collective-permute-done.22 = bf16[64,1024]{1,0:T(8,128)(2,1)S(1)} collective-permute-done((bf16[64,1024]{1,0:T(8,128)(2,1)S(1)}, bf16[64,1024]{1,0:T(8,128)(2,1)S(1)}, u32[]{:S(2)}, u32[]{:S(2)}) %collective-permute-start.22) | collective-permute-done | bytes 131104 | tf_op jit(solution)/shard_map/ppermute | solution.py:111
  68.5 4.1 %collective-permute-done.23 = bf16[64,1024]{1,0:T(8,128)(2,1)S(1)} collective-permute-done((bf16[64,1024]{1,0:T(8,128)(2,1)S(1)}, bf16[64,1024]{1,0:T(8,128)(2,1)S(1)}, u32[]{:S(2)}, u32[]{:S(2)}) %collective-permute-start.23) | collective-permute-done | bytes 131104 | tf_op jit(solution)/shard_map/ppermute | solution.py:111
  82.1 2.8 %collective-permute-start.27 = (bf16[64,1024]{1,0:T(8,128)(2,1)S(1)}, bf16[64,1024]{1,0:T(8,128)(2,1)S(1)}, u32[]{:S(2)}, u32[]{:S(2)}) collective-permute-start(bf16[64,1024]{1,0:T(8,128)(2,1)S(1)} %fusion.54), channel_id=1, source_target_pairs={{0,3},{1,2},{2,1},{3,0},{4,7},{5,6},{6,5},{7,4},{8,11},{9,10},{10,... | collective-permute-start | bytes 393224 | tf_op jit(solution)/shard_map/ppermute | solution.py:111
  91.3 2.7 %collective-permute-start.32 = (bf16[64,1024]{1,0:T(8,128)(2,1)S(1)}, bf16[64,1024]{1,0:T(8,128)(2,1)S(1)}, u32[]{:S(2)}, u32[]{:S(2)}) collective-permute-start(bf16[64,1024]{1,0:T(8,128)(2,1)S(1)} %get-tuple-element.21), channel_id=1, source_target_pairs={{0,3},{1,2},{2,1},{3,0},{4,7},{5,6},{6,5},{7,4},{8,11},{9,10},{10,... | collective-permute-start | bytes 393224 | tf_op jit(solution)/shard_map/ppermute | solution.py:111
  95.1 3.5 %collective-permute-done.32 = bf16[64,1024]{1,0:T(8,128)(2,1)S(1)} collective-permute-done((bf16[64,1024]{1,0:T(8,128)(2,1)S(1)}, bf16[64,1024]{1,0:T(8,128)(2,1)S(1)}, u32[]{:S(2)}, u32[]{:S(2)}) %collective-permute-start.32) | collective-permute-done | bytes 131104 | tf_op jit(solution)/shard_map/ppermute | solution.py:111
  98.7 4.9 %collective-permute-done.33 = bf16[64,1024]{1,0:T(8,128)(2,1)S(1)} collective-permute-done((bf16[64,1024]{1,0:T(8,128)(2,1)S(1)}, bf16[64,1024]{1,0:T(8,128)(2,1)S(1)}, u32[]{:S(2)}, u32[]{:S(2)}) %collective-permute-start.33) | collective-permute-done | bytes 131104 | tf_op jit(solution)/shard_map/ppermute | solution.py:111
  122.6 2.8 %collective-permute-start.50 = (bf16[64,1024]{1,0:T(8,128)(2,1)S(1)}, bf16[64,1024]{1,0:T(8,128)(2,1)S(1)}, u32[]{:S(2)}, u32[]{:S(2)}) collective-permute-start(bf16[64,1024]{1,0:T(8,128)(2,1)S(1)} %get-tuple-element.17), channel_id=1, source_target_pairs={{0,3},{1,2},{2,1},{3,0},{4,7},{5,6},{6,5},{7,4},{8,11},{9,10},{10,... | collective-permute-start | bytes 393224 | tf_op jit(solution)/shard_map/ppermute | solution.py:111
  130.8 4.4 %collective-permute-done.51 = bf16[64,1024]{1,0:T(8,128)(2,1)S(1)} collective-permute-done((bf16[64,1024]{1,0:T(8,128)(2,1)S(1)}, bf16[64,1024]{1,0:T(8,128)(2,1)S(1)}, u32[]{:S(2)}, u32[]{:S(2)}) %collective-permute-start.51) | collective-permute-done | bytes 131104 | tf_op jit(solution)/shard_map/ppermute | solution.py:111
  158.2 3.1 %collective-permute-done.60 = bf16[64,1024]{1,0:T(8,128)(2,1)S(1)} collective-permute-done((bf16[64,1024]{1,0:T(8,128)(2,1)S(1)}, bf16[64,1024]{1,0:T(8,128)(2,1)S(1)}, u32[]{:S(2)}, u32[]{:S(2)}) %collective-permute-start.60) | collective-permute-done | bytes 131104 | tf_op jit(solution)/shard_map/ppermute | solution.py:111
  165.4 4.3 %collective-permute-done.69 = bf16[64,1024]{1,0:T(8,128)(2,1)S(1)} collective-permute-done((bf16[64,1024]{1,0:T(8,128)(2,1)S(1)}, bf16[64,1024]{1,0:T(8,128)(2,1)S(1)}, u32[]{:S(2)}, u32[]{:S(2)}) %collective-permute-start.69) | collective-permute-done | bytes 131104 | tf_op jit(solution)/shard_map/ppermute | solution.py:111
  172.2 4.5 %collective-permute-done.70 = bf16[64,1024]{1,0:T(8,128)(2,1)S(1)} collective-permute-done((bf16[64,1024]{1,0:T(8,128)(2,1)S(1)}, bf16[64,1024]{1,0:T(8,128)(2,1)S(1)}, u32[]{:S(2)}, u32[]{:S(2)}) %collective-permute-start.70) | collective-permute-done | bytes 131104 | tf_op jit(solution)/shard_map/ppermute | solution.py:111
  180.8 4.2 %collective-permute-done.72 = bf16[64,1024]{1,0:T(8,128)(2,1)S(1)} collective-permute-done((bf16[64,1024]{1,0:T(8,128)(2,1)S(1)}, bf16[64,1024]{1,0:T(8,128)(2,1)S(1)}, u32[]{:S(2)}, u32[]{:S(2)}) %collective-permute-start.72) | collective-permute-done | bytes 131104 | tf_op jit(solution)/shard_map/ppermute | solution.py:111
  185.1 4.9 %collective-permute-done.73 = bf16[64,1024]{1,0:T(8,128)(2,1)S(1)} collective-permute-done((bf16[64,1024]{1,0:T(8,128)(2,1)S(1)}, bf16[64,1024]{1,0:T(8,128)(2,1)S(1)}, u32[]{:S(2)}, u32[]{:S(2)}) %collective-permute-start.73) | collective-permute-done | bytes 131104 | tf_op jit(solution)/shard_map/ppermute | solution.py:111
  194.7 2.8 %collective-permute-done.63 = bf16[64,1024]{1,0:T(8,128)(2,1)S(1)} collective-permute-done((bf16[64,1024]{1,0:T(8,128)(2,1)S(1)}, bf16[64,1024]{1,0:T(8,128)(2,1)S(1)}, u32[]{:S(2)}, u32[]{:S(2)}) %collective-permute-start.63) | collective-permute-done | bytes 131104 | tf_op jit(solution)/shard_map/ppermute | solution.py:81
  (280 shorter events, 108.7 us)
Async XLA Ops:
  9.4 13.7 %collective-permute-start.16 = (bf16[64,1024]{1,0:T(8,128)(2,1)S(1)}, bf16[64,1024]{1,0:T(8,128)(2,1)S(1)}, u32[]{:S(2)}, u32[]{:S(2)}) collective-permute-start(bf16[64,1024]{1,0:T(8,128)(2,1)S(1)} %bitcast.440), channel_id=1, source_target_pairs={{0,8},{4,12},{8,0},{12,4},{1,9},{5,13},{9,1},{13,5},{2,10},{6,14},... | collective-permute-start | bytes 393224 | tf_op jit(solution)/shard_map/ppermute | solution.py:81
  14.5 8.7 %collective-permute-start.2 = (bf16[64,1024]{1,0:T(8,128)(2,1)}, bf16[64,1024]{1,0:T(8,128)(2,1)S(1)}, u32[]{:S(2)}, u32[]{:S(2)}) collective-permute-start(bf16[64,1024]{1,0:T(8,128)(2,1)} %get-tuple-element.58), channel_id=1, source_target_pairs={{0,1},{1,0},{2,3},{3,2},{4,5},{5,4},{6,7},{7,6},{8,9},{9,8},{10,11... | collective-permute-start | bytes 393224 | tf_op jit(solution)/shard_map/ppermute | solution.py:111
  23.1 18.8 %collective-permute-start.17 = (bf16[2,64,1024]{2,1,0:T(8,128)(2,1)S(1)}, bf16[2,64,1024]{2,1,0:T(8,128)(2,1)S(1)}, u32[]{:S(2)}, u32[]{:S(2)}) collective-permute-start(bf16[2,64,1024]{2,1,0:T(8,128)(2,1)S(1)} %bitcast_dynamic-update-slice_fusion.44), channel_id=1, source_target_pairs={{0,4},{4,0},{8,12},{12,8},{1,5},{5,1},{9,13},{13,9},{2,6},{6,2},{1... | collective-permute-start | bytes 786440 | tf_op jit(solution)/shard_map/ppermute | solution.py:88
  26.5 9.0 %collective-permute-start.5 = (bf16[64,1024]{1,0:T(8,128)(2,1)S(1)}, bf16[64,1024]{1,0:T(8,128)(2,1)S(1)}, u32[]{:S(2)}, u32[]{:S(2)}) collective-permute-start(bf16[64,1024]{1,0:T(8,128)(2,1)S(1)} %get-tuple-element.35), channel_id=1, source_target_pairs={{0,1},{1,0},{2,3},{3,2},{4,5},{5,4},{6,7},{7,6},{8,9},{9,8},{10,11... | collective-permute-start | bytes 393224 | tf_op jit(solution)/shard_map/ppermute | solution.py:111
  44.0 15.3 %collective-permute-start.18 = (bf16[64,1024]{1,0:T(8,128)(2,1)S(1)}, bf16[64,1024]{1,0:T(8,128)(2,1)S(1)}, u32[]{:S(2)}, u32[]{:S(2)}) collective-permute-start(bf16[64,1024]{1,0:T(8,128)(2,1)S(1)} %get-tuple-element.42), channel_id=1, source_target_pairs={{0,1},{1,0},{2,3},{3,2},{4,5},{5,4},{6,7},{7,6},{8,9},{9,8},{10,11... | collective-permute-start | bytes 393224 | tf_op jit(solution)/shard_map/ppermute | solution.py:111
  50.3 9.0 %collective-permute-start.20 = (bf16[64,1024]{1,0:T(8,128)(2,1)S(1)}, bf16[64,1024]{1,0:T(8,128)(2,1)S(1)}, u32[]{:S(2)}, u32[]{:S(2)}) collective-permute-start(bf16[64,1024]{1,0:T(8,128)(2,1)S(1)} %fusion.55), channel_id=1, source_target_pairs={{0,3},{1,2},{2,1},{3,0},{4,7},{5,6},{6,5},{7,4},{8,11},{9,10},{10,... | collective-permute-start | bytes 393224 | tf_op jit(solution)/shard_map/ppermute | solution.py:111
  59.4 9.0 %collective-permute-start.21 = (bf16[64,1024]{1,0:T(8,128)(2,1)S(1)}, bf16[64,1024]{1,0:T(8,128)(2,1)S(1)}, u32[]{:S(2)}, u32[]{:S(2)}) collective-permute-start(bf16[64,1024]{1,0:T(8,128)(2,1)S(1)} %get-tuple-element.31), channel_id=1, source_target_pairs={{0,1},{1,0},{2,3},{3,2},{4,5},{5,4},{6,7},{7,6},{8,9},{9,8},{10,11... | collective-permute-start | bytes 393224 | tf_op jit(solution)/shard_map/ppermute | solution.py:111
  59.6 8.0 %collective-permute-start.22 = (bf16[64,1024]{1,0:T(8,128)(2,1)S(1)}, bf16[64,1024]{1,0:T(8,128)(2,1)S(1)}, u32[]{:S(2)}, u32[]{:S(2)}) collective-permute-start(bf16[64,1024]{1,0:T(8,128)(2,1)S(1)} %get-tuple-element.31), channel_id=1, source_target_pairs={{0,3},{1,2},{2,1},{3,0},{4,7},{5,6},{6,5},{7,4},{8,11},{9,10},{10,... | collective-permute-start | bytes 393224 | tf_op jit(solution)/shard_map/ppermute | solution.py:111
  63.3 10.7 %collective-permute-start.15 = (bf16[4,32,2048]{2,1,0:T(8,128)(2,1)S(1)}, bf16[4,32,2048]{2,1,0:T(8,128)(2,1)S(1)}, u32[]{:S(2)}, u32[]{:S(2)}) collective-permute-start(bf16[4,32,2048]{2,1,0:T(8,128)(2,1)S(1)} %bitcast_dynamic-update-slice_fusion.45), channel_id=1, source_target_pairs={{0,4},{4,0},{8,12},{12,8},{1,5},{5,1},{9,13},{13,9},{2,6},{6,2},{1... | collective-permute-start | bytes 1572872 | tf_op jit(solution)/shard_map/ppermute | solution.py:88
  80.8 9.1 %collective-permute-start.25 = (bf16[64,1024]{1,0:T(8,128)(2,1)S(1)}, bf16[64,1024]{1,0:T(8,128)(2,1)S(1)}, u32[]{:S(2)}, u32[]{:S(2)}) collective-permute-start(bf16[64,1024]{1,0:T(8,128)(2,1)S(1)} %get-tuple-element.40), channel_id=1, source_target_pairs={{0,1},{1,0},{2,3},{3,2},{4,5},{5,4},{6,7},{7,6},{8,9},{9,8},{10,11... | collective-permute-start | bytes 393224 | tf_op jit(solution)/shard_map/ppermute | solution.py:111
  82.1 7.8 %collective-permute-start.27 = (bf16[64,1024]{1,0:T(8,128)(2,1)S(1)}, bf16[64,1024]{1,0:T(8,128)(2,1)S(1)}, u32[]{:S(2)}, u32[]{:S(2)}) collective-permute-start(bf16[64,1024]{1,0:T(8,128)(2,1)S(1)} %fusion.54), channel_id=1, source_target_pairs={{0,3},{1,2},{2,1},{3,0},{4,7},{5,6},{6,5},{7,4},{8,11},{9,10},{10,... | collective-permute-start | bytes 393224 | tf_op jit(solution)/shard_map/ppermute | solution.py:111
  90.1 8.6 %collective-permute-start.31 = (bf16[64,1024]{1,0:T(8,128)(2,1)S(1)}, bf16[64,1024]{1,0:T(8,128)(2,1)S(1)}, u32[]{:S(2)}, u32[]{:S(2)}) collective-permute-start(bf16[64,1024]{1,0:T(8,128)(2,1)S(1)} %get-tuple-element.21), channel_id=1, source_target_pairs={{0,1},{1,0},{2,3},{3,2},{4,5},{5,4},{6,7},{7,6},{8,9},{9,8},{10,11... | collective-permute-start | bytes 393224 | tf_op jit(solution)/shard_map/ppermute | solution.py:111
  94.8 10.2 %collective-permute-start.45 = (bf16[4,32,2048]{2,1,0:T(8,128)(2,1)S(1)}, bf16[4,32,2048]{2,1,0:T(8,128)(2,1)S(1)}, u32[]{:S(2)}, u32[]{:S(2)}) collective-permute-start(bf16[4,32,2048]{2,1,0:T(8,128)(2,1)S(1)} %bitcast_dynamic-update-slice_fusion.28), channel_id=1, source_target_pairs={{0,4},{4,0},{8,12},{12,8},{1,5},{5,1},{9,13},{13,9},{2,6},{6,2},{1... | collective-permute-start | bytes 1572872 | tf_op jit(solution)/shard_map/ppermute | solution.py:88
  107.1 15.0 %collective-permute-start.46 = (bf16[64,1024]{1,0:T(8,128)(2,1)S(1)}, bf16[64,1024]{1,0:T(8,128)(2,1)S(1)}, u32[]{:S(2)}, u32[]{:S(2)}) collective-permute-start(bf16[64,1024]{1,0:T(8,128)(2,1)S(1)} %get-tuple-element.38), channel_id=1, source_target_pairs={{0,1},{1,0},{2,3},{3,2},{4,5},{5,4},{6,7},{7,6},{8,9},{9,8},{10,11... | collective-permute-start | bytes 393224 | tf_op jit(solution)/shard_map/ppermute | solution.py:111
  113.4 8.6 %collective-permute-start.48 = (bf16[64,1024]{1,0:T(8,128)(2,1)S(1)}, bf16[64,1024]{1,0:T(8,128)(2,1)S(1)}, u32[]{:S(2)}, u32[]{:S(2)}) collective-permute-start(bf16[64,1024]{1,0:T(8,128)(2,1)S(1)} %fusion.43), channel_id=1, source_target_pairs={{0,3},{1,2},{2,1},{3,0},{4,7},{5,6},{6,5},{7,4},{8,11},{9,10},{10,... | collective-permute-start | bytes 393224 | tf_op jit(solution)/shard_map/ppermute | solution.py:111
  122.2 8.6 %collective-permute-start.49 = (bf16[64,1024]{1,0:T(8,128)(2,1)S(1)}, bf16[64,1024]{1,0:T(8,128)(2,1)S(1)}, u32[]{:S(2)}, u32[]{:S(2)}) collective-permute-start(bf16[64,1024]{1,0:T(8,128)(2,1)S(1)} %get-tuple-element.17), channel_id=1, source_target_pairs={{0,1},{1,0},{2,3},{3,2},{4,5},{5,4},{6,7},{7,6},{8,9},{9,8},{10,11... | collective-permute-start | bytes 393224 | tf_op jit(solution)/shard_map/ppermute | solution.py:111
  127.3 9.3 %collective-permute-start.41 = (bf16[4,32,2048]{2,1,0:T(8,128)(2,1)S(1)}, bf16[4,32,2048]{2,1,0:T(8,128)(2,1)S(1)}, u32[]{:S(2)}, u32[]{:S(2)}) collective-permute-start(bf16[4,32,2048]{2,1,0:T(8,128)(2,1)S(1)} %bitcast_dynamic-update-slice_fusion.32), channel_id=1, source_target_pairs={{0,4},{4,0},{8,12},{12,8},{1,5},{5,1},{9,13},{13,9},{2,6},{6,2},{1... | collective-permute-start | bytes 1572872 | tf_op jit(solution)/shard_map/ppermute | solution.py:88
  140.5 8.2 %collective-permute-start.57 = (bf16[32,2048]{1,0:T(8,128)(2,1)S(1)}, bf16[32,2048]{1,0:T(8,128)(2,1)S(1)}, u32[]{:S(2)}, u32[]{:S(2)}) collective-permute-start(bf16[32,2048]{1,0:T(8,128)(2,1)S(1)} %get-tuple-element.48), channel_id=1, source_target_pairs={{0,16},{4,20},{8,24},{12,28},{16,0},{20,4},{24,8},{28,12},{1,17},{... | collective-permute-start | bytes 393224 | tf_op jit(solution)/shard_map/ppermute | solution.py:91
  143.2 9.3 %collective-permute-start.53 = (bf16[64,1024]{1,0:T(8,128)(2,1)S(1)}, bf16[64,1024]{1,0:T(8,128)(2,1)S(1)}, u32[]{:S(2)}, u32[]{:S(2)}) collective-permute-start(bf16[64,1024]{1,0:T(8,128)(2,1)S(1)} %get-tuple-element.36), channel_id=1, source_target_pairs={{0,1},{1,0},{2,3},{3,2},{4,5},{5,4},{6,7},{7,6},{8,9},{9,8},{10,11... | collective-permute-start | bytes 393224 | tf_op jit(solution)/shard_map/ppermute | solution.py:111
  150.0 7.8 %collective-permute-start.65 = (bf16[32,2048]{1,0:T(8,128)(2,1)S(1)}, bf16[32,2048]{1,0:T(8,128)(2,1)S(1)}, u32[]{:S(2)}, u32[]{:S(2)}) collective-permute-start(bf16[32,2048]{1,0:T(8,128)(2,1)S(1)} %get-tuple-element.12), channel_id=1, source_target_pairs={{0,16},{4,20},{8,24},{12,28},{16,0},{20,4},{24,8},{28,12},{1,17},{... | collective-permute-start | bytes 393224 | tf_op jit(solution)/shard_map/ppermute | solution.py:91
  152.6 9.2 %collective-permute-start.59 = (bf16[64,1024]{1,0:T(8,128)(2,1)S(1)}, bf16[64,1024]{1,0:T(8,128)(2,1)S(1)}, u32[]{:S(2)}, u32[]{:S(2)}) collective-permute-start(bf16[64,1024]{1,0:T(8,128)(2,1)S(1)} %get-tuple-element.5), channel_id=1, source_target_pairs={{0,1},{1,0},{2,3},{3,2},{4,5},{5,4},{6,7},{7,6},{8,9},{9,8},{10,11... | collective-permute-start | bytes 393224 | tf_op jit(solution)/shard_map/ppermute | solution.py:111
  161.3 10.9 %collective-permute-start.61 = (bf16[64,1024]{1,0:T(8,128)(2,1)S(1)}, bf16[64,1024]{1,0:T(8,128)(2,1)S(1)}, u32[]{:S(2)}, u32[]{:S(2)}) collective-permute-start(bf16[64,1024]{1,0:T(8,128)(2,1)S(1)} %collective-permute-done.60), channel_id=1, source_target_pairs={{0,1},{1,0},{2,3},{3,2},{4,5},{5,4},{6,7},{7,6},{8,9},{9,8},{10,11... | collective-permute-start | bytes 393224 | tf_op jit(solution)/shard_map/ppermute | solution.py:111
  176.9 8.2 %collective-permute-start.71 = (bf16[64,1024]{1,0:T(8,128)(2,1)S(1)}, bf16[64,1024]{1,0:T(8,128)(2,1)S(1)}, u32[]{:S(2)}, u32[]{:S(2)}) collective-permute-start(bf16[64,1024]{1,0:T(8,128)(2,1)S(1)} %get-tuple-element.10), channel_id=1, source_target_pairs={{0,1},{1,0},{2,3},{3,2},{4,5},{5,4},{6,7},{7,6},{8,9},{9,8},{10,11... | collective-permute-start | bytes 393224 | tf_op jit(solution)/shard_map/ppermute | solution.py:111
  180.7 10.2 %collective-permute-start.62 = (bf16[2,64,1024]{2,1,0:T(8,128)(2,1)S(1)}, bf16[2,64,1024]{2,1,0:T(8,128)(2,1)S(1)}, u32[]{:S(2)}, u32[]{:S(2)}) collective-permute-start(bf16[2,64,1024]{2,1,0:T(8,128)(2,1)S(1)} %fusion.29), channel_id=1, source_target_pairs={{0,4},{4,0},{8,12},{12,8},{1,5},{5,1},{9,13},{13,9},{2,6},{6,2},{1... | collective-permute-start | bytes 786440 | tf_op jit(solution)/shard_map/ppermute | solution.py:88
  (60 other events, 399.1 us)
